TPU v7x, 256 devices: a whole 4x4x8 slice. The times are simulated.
256 devices in a mesh: group: 8 (over z), fsdp: 32 (over x, y, core).
Axes of the slice: x: 4, y: 4, z: 8, core: 2. Of those that a mesh axis runs over, the one named last changes fastest.
Arguments:
- grad: bfloat16 [256, 262144], P(None, ('group', 'fsdp')), may hold values from -60 to 60
- moment: float32 [256, 262144], P(None, ('group', 'fsdp')), may hold values from 0.1 to 10
- order: int32 [256], replicated, may hold values from 0 to 255, each once
- left_stat: float32 [256, 512, 512], P(('group', 'fsdp')), may hold values from -5 to 5
- right_stat: float32 [256, 512, 512], P(('group', 'fsdp')), may hold values from -5 to 5
- left_root: bfloat16 [256, 512, 512], P(('group', 'fsdp')), may hold values from -2 to 2
- right_root: bfloat16 [256, 512, 512], P(('group', 'fsdp')), may hold values from -2 to 2
Outputs:
- update: bfloat16 [256, 262144], P(None, ('group', 'fsdp'))
- moment_new: float32 [256, 262144], P(None, ('group', 'fsdp'))
- left_new: float32 [256, 512, 512], P(('group', 'fsdp'))
- right_new: float32 [256, 512, 512], P(('group', 'fsdp'))
Inputs may be any that keep to these rules, and one draw needn't show every extreme that they name: `order`: every block is named by exactly one slot; slot s lies on the device of index s // 1 along group+fsdp.
All inputs are finite; a program needn't handle non-finite values.
Results may differ from a plain program's by a relative error of at most 0.0057.
Values may be sent and summed in bfloat16 or wider, within the bound.
A program may use at most 64 MiB of HBM per device.

v0:
```python
import jax
import jax.numpy as jnp
from jax import lax
from jax.sharding import PartitionSpec as P

MOMENT_DECAY = 0.95
STAT_DECAY = 0.9
ADAM_EPS = 1e-08
PRECON_EPS = 1e-06


def adam_squares(gradient, second):
    direction = gradient / (jnp.sqrt(second) + ADAM_EPS)
    return jnp.sum(direction * direction, axis=1)


def shards(grad, moment, order, left_stat, right_stat, left_root, right_root):
    group_count = lax.axis_size("group")
    fsdp_count = lax.axis_size("fsdp")
    block_count = grad.shape[0]
    per_device = left_stat.shape[0]
    side = left_stat.shape[1]
    gradient = grad.astype(jnp.float32)
    moment_new = MOMENT_DECAY * moment + (1.0 - MOMENT_DECAY) * gradient * gradient
    position = jnp.arange(block_count, dtype=jnp.int32)
    stride = group_count * per_device
    fsdp_index = position // stride
    inside = position % stride
    group_index = inside // per_device
    within = inside % per_device
    slot_index = (group_index * fsdp_count + fsdp_index) * per_device + within
    source = jnp.take(order, slot_index)
    outgoing = jnp.take(grad, source, axis=0)
    incoming = lax.all_to_all(
        lax.all_to_all(outgoing, "fsdp", split_axis=0, concat_axis=1, tiled=True),
        "group",
        split_axis=0,
        concat_axis=1,
        tiled=True,
    )
    blocks = incoming.reshape(per_device, side, side)
    gram_left = jnp.einsum("kij,klj->kil", blocks, blocks, preferred_element_type=jnp.float32)
    gram_right = jnp.einsum("kji,kjl->kil", blocks, blocks, preferred_element_type=jnp.float32)
    left_new = STAT_DECAY * left_stat + (1.0 - STAT_DECAY) * gram_left / side
    right_new = STAT_DECAY * right_stat + (1.0 - STAT_DECAY) * gram_right / side
    half = jnp.einsum("kij,kjl->kil", left_root, blocks, preferred_element_type=jnp.float32).astype(
        jnp.bfloat16
    )
    full = jnp.einsum("kij,kjl->kil", half, right_root, preferred_element_type=jnp.float32)
    precon_sq = jnp.sum(full * full, axis=(1, 2))
    precon = full.astype(jnp.bfloat16)
    returned = lax.all_to_all(
        lax.all_to_all(
            precon.reshape(per_device, side * side),
            "group",
            split_axis=1,
            concat_axis=0,
            tiled=True,
        ),
        "fsdp",
        split_axis=1,
        concat_axis=0,
        tiled=True,
    )
    inverse = jnp.zeros((block_count,), jnp.int32).at[source].set(position)
    arranged = jnp.take(returned, inverse, axis=0)
    device = lax.axis_index(("group", "fsdp"))
    my_blocks = lax.dynamic_slice_in_dim(order, device * per_device, per_device)
    placed = jnp.zeros((block_count,), jnp.float32).at[my_blocks].set(precon_sq)
    adam_total, precon_total = lax.psum(
        (adam_squares(gradient, moment_new), placed), ("group", "fsdp")
    )
    factor = jnp.sqrt(adam_total) / (jnp.sqrt(precon_total) + PRECON_EPS)
    widened = lax.optimization_barrier(arranged).astype(jnp.float32)
    update = (widened * factor[:, None]).astype(jnp.bfloat16)
    return (update, moment_new, left_new, right_new)


def solution(mesh):
    placed = (
        P(None, ("group", "fsdp")),
        P(None, ("group", "fsdp")),
        P(),
        P(("group", "fsdp"), None, None),
        P(("group", "fsdp"), None, None),
        P(("group", "fsdp"), None, None),
        P(("group", "fsdp"), None, None),
    )
    return jax.shard_map(
        shards,
        mesh=mesh,
        in_specs=placed,
        out_specs=(
            P(None, ("group", "fsdp")),
            P(None, ("group", "fsdp")),
            P(("group", "fsdp"), None, None),
            P(("group", "fsdp"), None, None),
        ),
        check_vma=False,
    )
```

profile of v0, /device:TPU:1, one launch (start us, length us, event | category | flops | bytes accessed | tf_op | source)
XLA Modules:
  0.0 173.0 jit_solution(12702737682411099035)
XLA Ops:
  0.6 0.0 copy-start
  0.7 0.0 copy-start.1
  0.7 0.7 copy-done.1
  1.4 0.0 copy-start.2
  1.4 1.9 %gather_fusion = s32[256]{0:T(256)S(1)} fusion(s32[256]{0:T(256)S(1)} %copy-done.1, s32[1024]{0:T(1024)S(1)} %pad_clamp_fusion.2), kind=kCustom, calls=%fused_computation.2 | custom fusion | bytes 3072 | tf_op jit(solution)/shard_map/jit(_take)/gather | solution.py:32
  3.4 0.0 copy-done.2
  3.4 1.2 gather_fusion.1
  4.6 0.1 select_bitcast_fusion
  4.7 20.0 %all_to_all.62 = bf16[32,8,1024]{2,1,0:T(8,128)(2,1)S(1)} all-to-all(bf16[32,8,1024]{2,1,0:T(8,128)(2,1)S(1)} %select_bitcast_fusion), channel_id=1, replica_groups=mesh['group'=8,'fsdp'=32] {'fsdp'}, dimensions={0} | all-to-all | bytes 1048576 | tf_op jit(solution)/shard_map/all_to_all | solution.py:35
  24.7 0.5 broadcast.363
  25.2 1.0 reduce.7
  26.2 1.2 reshape.239
  27.4 8.2 %all-to-all-start.1 = ((bf16[8,2,16384]{2,1,0:T(2,128)(2,1)}), bf16[8,2,16384]{2,1,0:T(2,128)(2,1)S(1)}, u32[]{:S(2)}, u32[]{:S(2)}) async-start(bf16[8,2,16384]{2,1,0:T(2,128)(2,1)} %reshape.239), calls=%async_computation.1 | async-start | bytes 1048576 | tf_op jit(solution)/shard_map/all_to_all | solution.py:34
  35.6 0.7 compare_select_fusion.5
  36.3 1.4 scatter_custom_fusion
  37.7 16.0 %all-to-all-done.1 = bf16[8,2,16384]{2,1,0:T(2,128)(2,1)S(1)} async-done(((bf16[8,2,16384]{2,1,0:T(2,128)(2,1)}), bf16[8,2,16384]{2,1,0:T(2,128)(2,1)S(1)}, u32[]{:S(2)}, u32[]{:S(2)}) %all-to-all-start.1) | async-done | bytes 524320 | tf_op jit(solution)/shard_map/all_to_all | solution.py:34
  53.7 0.5 reshape.240
  54.2 3.3 %reduce.4 = bf16[8,32768]{1,0:T(8,128)(2,1)S(1)} reduce(bf16[8,1,32768]{2,1,0:T(2,128)(2,1)S(1)} %reshape.240, bf16[]{:T(256)} %constant.151), dimensions={1}, to_apply=%all_to_all.50.reduce_sub_computation | reduce | bytes 1048578 | tf_op jit(solution)/shard_map/all_to_all | solution.py:34
  57.5 0.0 copy-start.5
  57.5 0.2 reshape.193
  57.8 0.0 copy-done
  57.8 0.8 copy-done.5
  58.6 1.6 multiply_reduce_fusion
  60.2 0.3 all_to_all.57
  60.5 3.9 %reduce.8 = bf16[8,32768]{1,0:T(8,128)(2,1)S(1)} reduce(bf16[8,1,32768]{2,1,0:T(2,128)(2,1)S(1)} %bitcast.42, bf16[]{:T(256)} %broadcast.363), dimensions={1}, to_apply=%bitcast.29.reduce_sub_computation | reduce | bytes 1048578
  64.4 0.0 copy-start.3
  64.4 1.2 reshape.241
  65.6 3.7 %all-to-all-start.2 = ((bf16[8,2,16384]{2,1,0:T(2,128)(2,1)}), bf16[8,2,16384]{2,1,0:T(2,128)(2,1)S(1)}, u32[]{:S(2)}, u32[]{:S(2)}) async-start(bf16[8,2,16384]{2,1,0:T(2,128)(2,1)} %reshape.241), calls=%async_computation.2 | async-start | bytes 1048576 | tf_op jit(solution)/shard_map/all_to_all | solution.py:53
  69.3 0.0 copy-done.3
  69.3 1.5 fusion.7
  70.9 2.1 %fusion.17 = f32[256]{0:T(256)S(1)} fusion(f32[256]{0:T(256)S(1)} %broadcast_in_dim.25, s32[]{:T(128)} %bitcast.11, f32[1]{0:T(128)} %bitcast.10, s32[1]{0:T(128)} %compare_select_fusion.5), kind=kLoop, calls=%fused_computation.54 | loop fusion | flops 4 | bytes 524 | tf_op jit(solution)/shard_map/scatter | solution.py:69
  73.0 74.7 %all-reduce = (f32[256]{0:T(256)S(1)}, f32[256]{0:T(256)S(1)}) all-reduce(f32[256]{0:T(256)S(1)} %fusion.17, f32[256]{0:T(256)S(1)} %get-tuple-element.19), channel_id=1, replica_groups=mesh['group'=8,'fsdp'=32] {'group','fsdp'}, use_global_device_ids=true, to_apply=%region_4.6 | all-reduce | flops 512 | bytes 4096 | tf_op jit(solution)/shard_map/psum | solution.py:70
  147.7 2.7 %fusion.2 = f32[1,512,512]{2,1,0:T(8,128)} fusion(bf16[512,512]{1,0:T(8,128)(2,1)S(1)} %reshape.193, f32[1,512,512]{2,1,0:T(8,128)} %param.14), kind=kOutput, calls=%fused_computation.10 | convolution fusion | flops 269221888 | bytes 2621440 | tf_op jit(solution)/shard_map/kij,klj->kil/dot_general | solution.py:42
  150.3 0.0 all-to-all-done.2
  150.3 0.5 reshape.242
  150.9 3.8 %bitcast_reduce_fusion = bf16[8,32768]{1,0:T(8,128)(2,1)} fusion(bf16[8,1,32768]{2,1,0:T(2,128)(2,1)S(1)} %reshape.242), kind=kLoop, calls=%fused_computation.57 | loop fusion | bytes 1048576 | tf_op jit(solution)/shard_map/all_to_all | solution.py:53
  154.6 0.0 copy-start.4
  154.6 4.3 %all-to-all-start.3 = ((bf16[8,32,1024]{2,0,1:T(8,128)(2,1)}), bf16[8,32,1024]{2,0,1:T(8,128)(2,1)S(1)}, u32[]{:S(2)}, u32[]{:S(2)}) async-start(bf16[8,32,1024]{2,0,1:T(8,128)(2,1)} %bitcast.16), calls=%async_computation.3 | async-start | bytes 1048576 | tf_op jit(solution)/shard_map/all_to_all | solution.py:52
  159.0 0.0 copy-done.4
  159.0 1.5 fusion.3
  160.5 10.3 %all-to-all-done.3 = bf16[8,32,1024]{2,0,1:T(8,128)(2,1)S(1)} async-done(((bf16[8,32,1024]{2,0,1:T(8,128)(2,1)}), bf16[8,32,1024]{2,0,1:T(8,128)(2,1)S(1)}, u32[]{:S(2)}, u32[]{:S(2)}) %all-to-all-start.3) | async-done | bytes 524320 | tf_op jit(solution)/shard_map/all_to_all | solution.py:52
  170.7 1.2 gather_fusion.2
  171.9 0.1 broadcast_select_fusion
  172.0 0.9 multiply_convert_fusion
  (11 shorter events, 0.1 us)
Async XLA Ops:
  0.6 57.1 %copy-start = (bf16[1,512,512]{2,1,0:T(8,128)(2,1)S(1)}, bf16[1,512,512]{2,1,0:T(8,128)(2,1)}, u32[]{:S(2)}) copy-start(bf16[1,512,512]{2,1,0:T(8,128)(2,1)} %param.17) | copy-start | bytes 1572868
  0.7 0.7 copy-start.1
  1.4 2.0 %copy-start.2 = (bf16[256,1024]{1,0:T(8,128)(2,1)S(1)}, bf16[256,1024]{1,0:T(8,128)(2,1)}, u32[]{:S(2)}) copy-start(bf16[256,1024]{1,0:T(8,128)(2,1)} %param.11) | copy-start | bytes 1572868
  27.4 26.3 %all-to-all-start.1 = ((bf16[8,2,16384]{2,1,0:T(2,128)(2,1)}), bf16[8,2,16384]{2,1,0:T(2,128)(2,1)S(1)}, u32[]{:S(2)}, u32[]{:S(2)}) async-start(bf16[8,2,16384]{2,1,0:T(2,128)(2,1)} %reshape.239), calls=%async_computation.1 | async-start | bytes 1048576 | tf_op jit(solution)/shard_map/all_to_all | solution.py:34
  57.5 1.0 copy-start.5
  64.4 4.9 %copy-start.3 = (f32[256,1024]{1,0:T(8,128)S(1)}, f32[256,1024]{1,0:T(8,128)}, u32[]{:S(2)}) copy-start(f32[256,1024]{1,0:T(8,128)} %param.12) | copy-start | bytes 3145732
  65.6 84.7 %all-to-all-start.2 = ((bf16[8,2,16384]{2,1,0:T(2,128)(2,1)}), bf16[8,2,16384]{2,1,0:T(2,128)(2,1)S(1)}, u32[]{:S(2)}, u32[]{:S(2)}) async-start(bf16[8,2,16384]{2,1,0:T(2,128)(2,1)} %reshape.241), calls=%async_computation.2 | async-start | bytes 1048576 | tf_op jit(solution)/shard_map/all_to_all | solution.py:53
  154.6 4.4 %copy-start.4 = (f32[1,512,512]{2,1,0:T(8,128)S(1)}, f32[1,512,512]{2,1,0:T(8,128)}, u32[]{:S(2)}) copy-start(f32[1,512,512]{2,1,0:T(8,128)} %param.15) | copy-start | bytes 3145732
  154.6 16.1 %all-to-all-start.3 = ((bf16[8,32,1024]{2,0,1:T(8,128)(2,1)}), bf16[8,32,1024]{2,0,1:T(8,128)(2,1)S(1)}, u32[]{:S(2)}, u32[]{:S(2)}) async-start(bf16[8,32,1024]{2,0,1:T(8,128)(2,1)} %bitcast.16), calls=%async_computation.3 | async-start | bytes 1048576 | tf_op jit(solution)/shard_map/all_to_all | solution.py:52
where the time goes:
time: 174 us; the launch traced here: 173 us
  blocking collectives  94.7 us (54%)
  waiting for transfers between devices  26.2 us (15%)
  starting transfers between devices  16.2 us (9%)
  local copies, waits for them, and re-layouts  15.4 us (9%)
  other arithmetic  13.9 us (8%)
  matrix products  5.73 us (3%)
    psum x1, blocking collectives, shards(): lax.psum((adam_squares(gradient, moment_new), placed), ('group', 'fsdp'))  74.7 us
    all_to_all x1, blocking collectives, shards(): lax.all_to_all(outgoing, 'fsdp', split_axis=0, concat_axis=1, tiled=True)  20 us
    all_to_all x1, waiting for transfers between devices, shards(): lax.all_to_all(lax.all_to_all(outgoing, 'fsdp', split_axis=0, concat_axis...  16 us
    all_to_all x1, waiting for transfers between devices, shards(): lax.all_to_all(lax.all_to_all(precon.reshape(per_device, side * side), 'g...  10.3 us
    all_to_all x1, starting transfers between devices, shards(): lax.all_to_all(lax.all_to_all(outgoing, 'fsdp', split_axis=0, concat_axis...  8.19 us
    unnamed x16, local copies, waits for them, and re-layouts  4.92 us
    all_to_all x1, starting transfers between devices, shards(): lax.all_to_all(lax.all_to_all(precon.reshape(per_device, side * side), 'g...  4.34 us
    all_to_all x2, other arithmetic, shards(): lax.all_to_all(lax.all_to_all(outgoing, 'fsdp', split_axis=0, concat_axis...  4.32 us
  transfers between devices with their start and end apart: 3, of which 2 were waited for; matrix products, arithmetic and copies ran while one was open for 6% of the time, Pallas kernels for 0%

commit v1 on v0

v1 whole, which is shorter than its diff:
```python
import functools

import jax
import jax.numpy as jnp
from jax import lax
from jax.experimental import pallas as pl
from jax.experimental.pallas import tpu as pltpu
from jax.sharding import PartitionSpec as P

MOMENT_DECAY = 0.95
STAT_DECAY = 0.9
ADAM_EPS = 1e-08
PRECON_EPS = 1e-06

LANES = 128
SUBLANES = 8
MESH = pl.DeviceIdType.MESH


def matmul(a, b, a_dim=1, b_dim=0):
    return lax.dot_general(
        a, b, (((a_dim,), (b_dim,)), ((), ())), preferred_element_type=jnp.float32
    )


def widen(source, wide):
    depth, fan = source.shape[:2]
    step = min(fan, 32)
    for i in range(depth):
        for j in range(0, fan, step):
            part = source[i, j : j + step].astype(jnp.float32)
            start = (i * fan + j) * SUBLANES
            wide[start : start + step * SUBLANES, :] = part.reshape(step * SUBLANES, LANES)


def alternate(count):
    return sorted(range(1, count), key=lambda k: (-min(k, count - k), k))


def exchange(
    depth,
    across,
    grad_hbm,
    moment_hbm,
    order_hbm,
    left_stat_hbm,
    right_stat_hbm,
    left_root_hbm,
    right_root_hbm,
    landed_back,
    moment,
    left_stat,
    right_stat,
    order,
    grad,
    left_root,
    right_root,
    wide,
    sent,
    relay,
    landed,
    sent_back,
    relay_back,
    block,
    norms,
    norms_z,
    norms_z_sum,
    norms_f,
    load_sem,
    z_send,
    z_recv,
    f_send,
    f_recv,
    norm_send,
    norm_recv,
):
    fan = relay.shape[0]
    row = fan // across
    blocks = depth * fan
    side = block.shape[0]
    pieces = side // LANES
    g = lax.axis_index("group")
    f = lax.axis_index("fsdp")
    x = f // row
    me = g * fan + f

    loads = [
        pltpu.make_async_copy(source, target, load_sem.at[i])
        for i, (source, target) in enumerate(
            (
                (order_hbm, order),
                (grad_hbm, grad),
                (moment_hbm, moment),
                (left_root_hbm, left_root),
                (right_root_hbm, right_root),
                (left_stat_hbm, left_stat),
                (right_stat_hbm, right_stat),
            )
        )
    ]
    for load in loads:
        load.start()

    barrier = pltpu.get_barrier_semaphore()

    def greet_z(k, carry):
        pl.semaphore_signal(barrier, inc=1, device_id=((g + k) % depth, f), device_id_type=MESH)
        return carry

    def greet_f(k, carry):
        pl.semaphore_signal(barrier, inc=1, device_id=(g, (f + k) % fan), device_id_type=MESH)
        return carry

    lax.fori_loop(1, depth, greet_z, 0)
    lax.fori_loop(1, fan, greet_f, 0)

    loads[0].wait()
    which = lax.broadcasted_iota(jnp.int32, (blocks, blocks), 0)
    holds = jnp.where(which == order[...], 1.0, 0.0)
    slots_half = holds.T.astype(jnp.bfloat16)

    def narrow(target):
        step = min(blocks, 32)
        for i in range(0, blocks, step):
            part = wide[i * SUBLANES : (i + step) * SUBLANES, :]
            target[i : i + step] = part.reshape(step, SUBLANES, LANES).astype(jnp.bfloat16)

    def chunk_of(k):
        return ((x + k) % across) * row

    def send_z(k, source, through, way):
        start = chunk_of(k)

        for j in alternate(depth):
            to = (g + j) % depth
            pltpu.make_async_remote_copy(
                src_ref=source.at[pl.ds(to * fan + start, row)],
                dst_ref=through.at[pl.ds(start, row), g],
                send_sem=z_send.at[way],
                recv_sem=z_recv.at[way, k],
                device_id=(to, f),
                device_id_type=MESH,
            ).start()
        pltpu.make_async_copy(
            source.at[pl.ds(g * fan + start, row)],
            through.at[pl.ds(start, row), g],
            z_recv.at[way, k],
        ).start()

    def send_f(k, through, target, way):
        start = chunk_of(k)
        arrived = through.at[pl.ds(start, row)]
        pltpu.make_async_copy(arrived, arrived, z_recv.at[way, k]).wait()
        place = f % row

        for j in alternate(row) + ([] if k == 0 else [0]):
            to = start + (place + j) % row
            pltpu.make_async_remote_copy(
                src_ref=through.at[to],
                dst_ref=target.at[:, f],
                send_sem=f_send.at[way],
                recv_sem=f_recv.at[way],
                device_id=(g, to),
                device_id_type=MESH,
            ).start()
        if k == 0:
            pltpu.make_async_copy(through.at[f], target.at[:, f], f_recv.at[way]).start()

    def wait_all(target, way):
        pltpu.make_async_copy(target, target, f_recv.at[way]).wait()

    def wait_sent(source, through, way):
        part = source.at[pl.ds(0, (depth - 1) * fan)]
        pltpu.make_async_copy(part, part, z_send.at[way]).wait()
        part = through.at[pl.ds(0, fan - 1)]
        pltpu.make_async_copy(part, part, f_send.at[way]).wait()

    chunks = sorted(range(across), key=lambda k: -min(k, across - k))

    loads[1].wait()
    for c in range(0, SUBLANES, 2):
        pair = matmul(slots_half, grad[:, c * LANES : (c + 2) * LANES])
        wide[pl.ds(c, blocks, stride=SUBLANES), :] = pair[:, :LANES]
        wide[pl.ds(c + 1, blocks, stride=SUBLANES), :] = pair[:, LANES:]
    narrow(sent)
    pl.semaphore_wait(barrier, depth - 1 + fan - 1)
    for k in chunks[:2]:
        send_z(k, sent, relay, 0)

    loads[2].wait()
    tall = min(blocks, 32)
    share = jnp.zeros((1, blocks), jnp.float32)
    for i in range(0, blocks, tall):
        rows = pl.ds(i, tall)
        gradient = grad[rows, :].astype(jnp.float32)
        second = MOMENT_DECAY * moment[rows, :] + (1.0 - MOMENT_DECAY) * gradient * gradient
        moment[rows, :] = second
        direction = gradient / (jnp.sqrt(second) + ADAM_EPS)
        squares = jnp.sum(direction * direction, axis=1, keepdims=True)
        share = share + jnp.sum(holds[i : i + tall, :] * squares, axis=0, keepdims=True)
    norms[...] = share
    for i, k in enumerate(chunks):
        send_f(k, relay, landed, 0)
        if i + 2 < across:
            send_z(chunks[i + 2], sent, relay, 0)

    def norm_z(j, carry):
        pltpu.make_async_remote_copy(
            src_ref=norms,
            dst_ref=norms_z.at[g],
            send_sem=norm_send.at[0],
            recv_sem=norm_recv.at[0],
            device_id=((g + j) % depth, f),
            device_id_type=MESH,
        ).start()
        return carry

    lax.fori_loop(1, depth, norm_z, 0)
    pltpu.make_async_copy(norms, norms_z.at[g], norm_recv.at[0]).start()
    pltpu.make_async_copy(norms_z, norms_z, norm_recv.at[0]).wait()
    norms_z_sum[...] = jnp.sum(norms_z[...], axis=0)

    def norm_f(j, carry):
        pltpu.make_async_remote_copy(
            src_ref=norms_z_sum,
            dst_ref=norms_f.at[f],
            send_sem=norm_send.at[1],
            recv_sem=norm_recv.at[1],
            device_id=(g, (f + j) % fan),
            device_id_type=MESH,
        ).start()
        return carry

    lax.fori_loop(1, fan, norm_f, 0)
    pltpu.make_async_copy(norms_z_sum, norms_f.at[f], norm_recv.at[1]).start()

    wait_all(landed, 0)
    widen(landed, wide)
    for c in range(pieces):
        block[:, c * LANES : (c + 1) * LANES] = wide[pl.ds(c, side, stride=pieces), :].astype(
            jnp.bfloat16
        )
    loads[3].wait()
    loads[4].wait()
    half = matmul(left_root[...], block[...]).astype(jnp.bfloat16)
    full = matmul(half, right_root[...])
    precon_sq = jnp.sum(full * full, keepdims=True)
    precon = full.astype(jnp.bfloat16).astype(jnp.float32)
    pltpu.make_async_copy(norms_f, norms_f, norm_recv.at[1]).wait()
    totals = jnp.sum(norms_f[...], axis=0)
    lane = lax.broadcasted_iota(jnp.int32, (1, blocks), 1)
    adam_sq = jnp.sum(jnp.where(lane == me, totals, 0.0), keepdims=True)
    scale = jnp.sqrt(adam_sq) / (jnp.sqrt(precon_sq) + PRECON_EPS)
    scaled = precon * scale
    for c in range(pieces):
        wide[pl.ds(c, side, stride=pieces), :] = scaled[:, c * LANES : (c + 1) * LANES]
    narrow(sent_back)

    for k in chunks[:2]:
        send_z(k, sent_back, relay_back, 1)
    loads[5].wait()
    left = matmul(block[...], block[...], 1, 1)
    left_stat[...] = STAT_DECAY * left_stat[...] + (1.0 - STAT_DECAY) * left / side
    loads[6].wait()
    right = matmul(block[...], block[...], 0, 0)
    right_stat[...] = STAT_DECAY * right_stat[...] + (1.0 - STAT_DECAY) * right / side
    for i, k in enumerate(chunks):
        send_f(k, relay_back, landed_back, 1)
        if i + 2 < across:
            send_z(chunks[i + 2], sent_back, relay_back, 1)
    wait_all(landed_back, 1)
    wait_sent(sent, relay, 0)
    wait_sent(sent_back, relay_back, 1)
    part = norms_z.at[pl.ds(0, depth - 1)]
    pltpu.make_async_copy(part, part, norm_send.at[0]).wait()
    part = norms_f.at[pl.ds(0, fan - 1)]
    pltpu.make_async_copy(part, part, norm_send.at[1]).wait()


def write(
    landed,
    moment,
    left_stat,
    right_stat,
    order_hbm,
    update_hbm,
    moment_hbm,
    left_hbm,
    right_hbm,
    order,
    wide,
    update,
    sems,
):
    load = pltpu.make_async_copy(order_hbm, order, sems.at[0])
    load.start()
    stores = [
        pltpu.make_async_copy(moment, moment_hbm, sems.at[1]),
        pltpu.make_async_copy(left_stat, left_hbm, sems.at[2]),
        pltpu.make_async_copy(right_stat, right_hbm, sems.at[3]),
    ]
    for store in stores:
        store.start()
    widen(landed, wide)
    load.wait()
    blocks = update.shape[0]
    which = lax.broadcasted_iota(jnp.int32, (blocks, blocks), 0)
    holds = jnp.where(which == order[...], 1.0, 0.0).astype(jnp.bfloat16)
    for c in range(0, SUBLANES, 2):
        pair = jnp.concatenate(
            [wide[pl.ds(c + i, blocks, stride=SUBLANES), :] for i in range(2)], axis=1
        ).astype(jnp.bfloat16)
        columns = pl.ds(c * LANES, 2 * LANES)
        update[:, columns] = matmul(holds, pair).astype(jnp.bfloat16)
        stores.append(
            pltpu.make_async_copy(update.at[:, columns], update_hbm.at[:, columns], sems.at[4 + c // 2])
        )
        stores[-1].start()
    for store in stores:
        store.wait()


def shards(across, grad, moment, order, left_stat, right_stat, left_root, right_root):
    depth = lax.axis_size("group")
    fan = lax.axis_size("fsdp")
    blocks, entries = grad.shape
    side = left_stat.shape[-1]
    f32, bf16 = jnp.float32, jnp.bfloat16
    tile = (SUBLANES, LANES)
    hbm = pl.BlockSpec(memory_space=pltpu.HBM)
    vmem = pl.BlockSpec(memory_space=pltpu.VMEM)
    order = order.reshape(1, blocks)
    entry_shapes = jax.ShapeDtypeStruct((blocks, entries), f32)
    stat_shapes = jax.ShapeDtypeStruct((side, side), f32)
    landed, moment_new, left_new, right_new = pl.pallas_call(
        functools.partial(exchange, depth, across),
        out_shape=(
            jax.ShapeDtypeStruct((depth, fan, *tile), bf16),
            entry_shapes,
            stat_shapes,
            stat_shapes,
        ),
        in_specs=[hbm] * 7,
        out_specs=(vmem,) * 4,
        scratch_shapes=[
            pltpu.VMEM((1, blocks), jnp.int32),
            pltpu.VMEM((blocks, entries), bf16),
            pltpu.VMEM((side, side), bf16),
            pltpu.VMEM((side, side), bf16),
            pltpu.VMEM((blocks * SUBLANES, LANES), f32),
            pltpu.VMEM((blocks, *tile), bf16),
            pltpu.VMEM((fan, depth, *tile), bf16),
            pltpu.VMEM((depth, fan, *tile), bf16),
            pltpu.VMEM((blocks, *tile), bf16),
            pltpu.VMEM((fan, depth, *tile), bf16),
            pltpu.VMEM((side, side), bf16),
            pltpu.VMEM((1, blocks), f32),
            pltpu.VMEM((depth, 1, blocks), f32),
            pltpu.VMEM((1, blocks), f32),
            pltpu.VMEM((fan, 1, blocks), f32),
            pltpu.SemaphoreType.DMA((7,)),
            pltpu.SemaphoreType.DMA((2,)),
            pltpu.SemaphoreType.DMA((2, across)),
            pltpu.SemaphoreType.DMA((2,)),
            pltpu.SemaphoreType.DMA((2,)),
            pltpu.SemaphoreType.DMA((2,)),
            pltpu.SemaphoreType.DMA((2,)),
        ],
        compiler_params=pltpu.CompilerParams(
            collective_id=0, has_side_effects=True, vmem_limit_bytes=40 * 1024 * 1024
        ),
        cost_estimate=pl.CostEstimate(
            flops=8 * side**3 + 2 * blocks * blocks * entries,
            bytes_accessed=6 * blocks * entries + 12 * side * side,
            transcendentals=2 * blocks * entries,
        ),
    )(
        *(
            pltpu.with_memory_space_constraint(operand, pltpu.HBM)
            for operand in (
                grad,
                moment,
                order,
                left_stat[0],
                right_stat[0],
                left_root[0],
                right_root[0],
            )
        )
    )
    update, moment_new, left_new, right_new = pl.pallas_call(
        write,
        out_shape=(
            jax.ShapeDtypeStruct((blocks, entries), bf16),
            entry_shapes,
            stat_shapes,
            stat_shapes,
        ),
        in_specs=[vmem] * 4 + [hbm],
        out_specs=(hbm,) * 4,
        scratch_shapes=[
            pltpu.VMEM((1, blocks), jnp.int32),
            pltpu.VMEM((blocks * SUBLANES, LANES), f32),
            pltpu.VMEM((blocks, entries), bf16),
            pltpu.SemaphoreType.DMA((8,)),
        ],
        compiler_params=pltpu.CompilerParams(vmem_limit_bytes=40 * 1024 * 1024),
        cost_estimate=pl.CostEstimate(
            flops=2 * blocks * blocks * entries,
            bytes_accessed=6 * blocks * entries + 8 * side * side,
            transcendentals=0,
        ),
    )(
        landed,
        moment_new,
        left_new,
        right_new,
        pltpu.with_memory_space_constraint(order, pltpu.HBM),
    )
    return (update, moment_new, left_new[None], right_new[None])


def solution(mesh):
    across = 4 if mesh.shape["fsdp"] == 32 else 2
    placed = (
        P(None, ("group", "fsdp")),
        P(None, ("group", "fsdp")),
        P(),
        P(("group", "fsdp"), None, None),
        P(("group", "fsdp"), None, None),
        P(("group", "fsdp"), None, None),
        P(("group", "fsdp"), None, None),
    )
    return jax.shard_map(
        functools.partial(shards, across),
        mesh=mesh,
        in_specs=placed,
        out_specs=(
            P(None, ("group", "fsdp")),
            P(None, ("group", "fsdp")),
            P(("group", "fsdp"), None, None),
            P(("group", "fsdp"), None, None),
        ),
        check_vma=False,
    )
```

time: 174 us -> 55.4 us (0.32)
  blocking collectives: 94.7 us -> 0 us
  Pallas kernels: 0 us -> 54.7 us
  waiting for transfers between devices: 26.2 us -> 0 us
  starting transfers between devices: 16.2 us -> 0 us
  local copies, waits for them, and re-layouts: 15.4 us -> 0 us
  other arithmetic: 13.9 us -> 0 us
  matrix products: 5.73 us -> 0 us
    psum x1 -> x0, blocking collectives: 74.7 us -> none  [shards(): lax.psum((adam_squares(gradient, moment_new), placed), ('group', 'fsdp'))]
    pallas_call x0 -> x2, Pallas kernels: none -> 54.7 us  [the longest x1 52.8 us: shards(): pl.pallas_call(functools.partial(exchange, depth, across), out_shape=(jax...]
    all_to_all x3 -> x0, waiting for transfers between devices: 26.2 us -> none  [the longest x1 16 us: shards(): lax.all_to_all(lax.all_to_all(outgoing, 'fsdp', split_axis=0, concat_axis...]
    all_to_all x1 -> x0, blocking collectives: 20 us -> none  [shards(): lax.all_to_all(outgoing, 'fsdp', split_axis=0, concat_axis=1, tiled=True)]
    all_to_all x3 -> x0, starting transfers between devices: 16.2 us -> none  [the longest x1 8.19 us: shards(): lax.all_to_all(lax.all_to_all(outgoing, 'fsdp', split_axis=0, concat_axis...]
    dot_general x3 -> x0, matrix products: 5.73 us -> none  [the longest x1 2.67 us: shards(): jnp.einsum('kij,klj->kil', blocks, blocks, preferred_element_type=jnp.flo...]
    unnamed x16 -> x0, local copies, waits for them, and re-layouts: 4.92 us -> none
    all_to_all x3 -> x0, local copies, waits for them, and re-layouts: 4.58 us -> none  [the longest x2 4.07 us: shards(): lax.all_to_all(precon.reshape(per_device, side * side), 'group', split_ax...]
  transfers between devices with their start and end apart: 3 -> 0, of which waited for: 2 -> 0; matrix products, arithmetic and copies ran while one was open for 6% -> 0% of each run, Pallas kernels for 0% -> 0%
where the time goes in v1:
time: 55.4 us; the launch traced here: 55.3 us
  Pallas kernels  54.7 us (99%)
  between operations  0.64 us (1%)
    pallas_call x1, Pallas kernels, shards(): pl.pallas_call(functools.partial(exchange, depth, across), out_shape=(jax...  52.8 us
    pallas_call x1, Pallas kernels, shards(): pl.pallas_call(write, out_shape=(jax.ShapeDtypeStruct((blocks, entries),...  1.89 us

profile of v1, /device:TPU:1, one launch (start us, length us, event | category | flops | bytes accessed | tf_op | source)
XLA Modules:
  0.0 55.3 jit_solution(8213140047814163261)
XLA Ops:
  0.6 52.8 %shard_map.102 = (bf16[8,32,8,128]{3,2,1,0:T(8,128)(2,1)S(1)}, f32[256,1024]{1,0:T(8,128)S(1)}, f32[512,512]{1,0:T(8,128)S(1)}, f32[512,512]{1,0:T(8,128)S(1)}) custom-call(bf16[256,1024]{1,0:T(8,128)(2,1)} %grad_hbm.1, f32[256,1024]{1,0:T(8,128)} %moment_hbm.1, s32[1,256]{1,0:T(1,128)} %bitcast.11, f32[512,512]{1,0:T(8,128)} %bitcast.7, ...), custom_call_target="tpu_custom_call" | custom-call | flops 1207959552 | bytes 4718592 | tf_op jit(solution)/shard_map/pallas_call | solution.py:335
  53.5 1.9 %shard_map.103 = (bf16[256,1024]{1,0:T(8,128)(2,1)}, f32[256,1024]{1,0:T(8,128)}, f32[512,512]{1,0:T(8,128)}, f32[512,512]{1,0:T(8,128)}) custom-call(bf16[8,32,8,128]{3,2,1,0:T(8,128)(2,1)S(1)} %get-tuple-element.12.landed, f32[256,1024]{1,0:T(8,128)S(1)} %get-tuple-element.13.moment, f32[512,512]{1,0:T(8,128)S(1)} %get-tuple-element.14.left_stat, ...), custom_call_target="tpu_custom_call" | custom-call | flops 134217728 | bytes 3670016 | tf_op jit(solution)/shard_map/pallas_call | solution.py:391

commit v2 on v1

--- a/solution.py
+++ b/solution.py
@@ -66,9 +66,12 @@
     norms_z,
     norms_z_sum,
     norms_f,
+    hop,
+    hop_back,
     load_sem,
     z_send,
     z_recv,
+    hop_recv,
     f_send,
     f_recv,
     norm_send,
@@ -83,6 +86,8 @@
     f = lax.axis_index("fsdp")
     x = f // row
     me = g * fan + f
+    hops = int(depth % 4 == 0)
+    leg = depth // 4 + f % 2 * (depth // 2)
 
     loads = [
         pltpu.make_async_copy(source, target, load_sem.at[i])
@@ -132,6 +137,8 @@
         start = chunk_of(k)
 
         for j in alternate(depth):
+            if hops and j == depth // 2:
+                continue
             to = (g + j) % depth
             pltpu.make_async_remote_copy(
                 src_ref=source.at[pl.ds(to * fan + start, row)],
@@ -147,6 +154,37 @@
             z_recv.at[way, k],
         ).start()
 
+    def send_hop(source, hop, way):
+        pltpu.make_async_remote_copy(
+            src_ref=source.at[pl.ds((g + depth // 2) % depth * fan, fan)],
+            dst_ref=hop,
+            send_sem=z_send.at[way],
+            recv_sem=hop_recv.at[way],
+            device_id=((g + leg) % depth, f),
+            device_id_type=MESH,
+        ).start()
+
+    def pass_on(hop, through, way):
+        pltpu.make_async_copy(hop, hop, hop_recv.at[way]).wait()
+        for k in chunks:
+            rows = pl.ds(chunk_of(k), row)
+            pltpu.make_async_remote_copy(
+                src_ref=hop.at[rows],
+                dst_ref=through.at[rows, (g + depth - leg) % depth],
+                send_sem=z_send.at[way],
+                recv_sem=z_recv.at[way, k],
+                device_id=((g + leg) % depth, f),
+                device_id_type=MESH,
+            ).start()
+
+    def send_z_all(source, hop, through, way):
+        if hops:
+            send_hop(source, hop, way)
+        for i, k in enumerate(chunks):
+            send_z(k, source, through, way)
+            if hops and i == 1:
+                pass_on(hop, through, way)
+
     def send_f(k, through, target, way):
         start = chunk_of(k)
         arrived = through.at[pl.ds(start, row)]
@@ -170,7 +208,7 @@
         pltpu.make_async_copy(target, target, f_recv.at[way]).wait()
 
     def wait_sent(source, through, way):
-        part = source.at[pl.ds(0, (depth - 1) * fan)]
+        part = source.at[pl.ds(0, (depth - 1 + hops) * fan)]
         pltpu.make_async_copy(part, part, z_send.at[way]).wait()
         part = through.at[pl.ds(0, fan - 1)]
         pltpu.make_async_copy(part, part, f_send.at[way]).wait()
@@ -184,8 +222,7 @@
         wide[pl.ds(c + 1, blocks, stride=SUBLANES), :] = pair[:, LANES:]
     narrow(sent)
     pl.semaphore_wait(barrier, depth - 1 + fan - 1)
-    for k in chunks[:2]:
-        send_z(k, sent, relay, 0)
+    send_z_all(sent, hop, relay, 0)
 
     loads[2].wait()
     tall = min(blocks, 32)
@@ -199,10 +236,8 @@
         squares = jnp.sum(direction * direction, axis=1, keepdims=True)
         share = share + jnp.sum(holds[i : i + tall, :] * squares, axis=0, keepdims=True)
     norms[...] = share
-    for i, k in enumerate(chunks):
+    for k in chunks:
         send_f(k, relay, landed, 0)
-        if i + 2 < across:
-            send_z(chunks[i + 2], sent, relay, 0)
 
     def norm_z(j, carry):
         pltpu.make_async_remote_copy(
@@ -256,18 +291,15 @@
         wide[pl.ds(c, side, stride=pieces), :] = scaled[:, c * LANES : (c + 1) * LANES]
     narrow(sent_back)
 
-    for k in chunks[:2]:
-        send_z(k, sent_back, relay_back, 1)
+    send_z_all(sent_back, hop_back, relay_back, 1)
     loads[5].wait()
     left = matmul(block[...], block[...], 1, 1)
     left_stat[...] = STAT_DECAY * left_stat[...] + (1.0 - STAT_DECAY) * left / side
     loads[6].wait()
     right = matmul(block[...], block[...], 0, 0)
     right_stat[...] = STAT_DECAY * right_stat[...] + (1.0 - STAT_DECAY) * right / side
-    for i, k in enumerate(chunks):
+    for k in chunks:
         send_f(k, relay_back, landed_back, 1)
-        if i + 2 < across:
-            send_z(chunks[i + 2], sent_back, relay_back, 1)
     wait_all(landed_back, 1)
     wait_sent(sent, relay, 0)
     wait_sent(sent_back, relay_back, 1)
@@ -358,9 +390,12 @@
             pltpu.VMEM((depth, 1, blocks), f32),
             pltpu.VMEM((1, blocks), f32),
             pltpu.VMEM((fan, 1, blocks), f32),
+            pltpu.VMEM((fan, *tile), bf16),
+            pltpu.VMEM((fan, *tile), bf16),
             pltpu.SemaphoreType.DMA((7,)),
             pltpu.SemaphoreType.DMA((2,)),
             pltpu.SemaphoreType.DMA((2, across)),
+            pltpu.SemaphoreType.DMA((2,)),
             pltpu.SemaphoreType.DMA((2,)),
             pltpu.SemaphoreType.DMA((2,)),
             pltpu.SemaphoreType.DMA((2,)),

time: 55.4 us -> 57 us (1.029)
  Pallas kernels: 54.7 us -> 56.2 us
    pallas_call x1, Pallas kernels: 52.8 us -> 54.3 us  [shards(): pl.pallas_call(functools.partial(exchange, depth, across), out_shape=(jax...]
where the time goes in v2:
time: 57 us; the launch traced here: 56.8 us
  Pallas kernels  56.2 us (99%)
  between operations  0.64 us (1%)
    pallas_call x1, Pallas kernels, shards(): pl.pallas_call(functools.partial(exchange, depth, across), out_shape=(jax...  54.3 us
    pallas_call x1, Pallas kernels, shards(): pl.pallas_call(write, out_shape=(jax.ShapeDtypeStruct((blocks, entries),...  1.89 us

profile of v2, /device:TPU:1, one launch (start us, length us, event | category | flops | bytes accessed | tf_op | source)
XLA Modules:
  0.0 56.8 jit_solution(18341123558321157419)
XLA Ops:
  0.6 54.3 %shard_map.102 = (bf16[8,32,8,128]{3,2,1,0:T(8,128)(2,1)S(1)}, f32[256,1024]{1,0:T(8,128)S(1)}, f32[512,512]{1,0:T(8,128)S(1)}, f32[512,512]{1,0:T(8,128)S(1)}) custom-call(bf16[256,1024]{1,0:T(8,128)(2,1)} %grad_hbm.1, f32[256,1024]{1,0:T(8,128)} %moment_hbm.1, s32[1,256]{1,0:T(1,128)} %bitcast.11, f32[512,512]{1,0:T(8,128)} %bitcast.7, ...), custom_call_target="tpu_custom_call" | custom-call | flops 1207959552 | bytes 4718592 | tf_op jit(solution)/shard_map/pallas_call | solution.py:367
  55.0 1.9 %shard_map.103 = (bf16[256,1024]{1,0:T(8,128)(2,1)}, f32[256,1024]{1,0:T(8,128)}, f32[512,512]{1,0:T(8,128)}, f32[512,512]{1,0:T(8,128)}) custom-call(bf16[8,32,8,128]{3,2,1,0:T(8,128)(2,1)S(1)} %get-tuple-element.12.landed, f32[256,1024]{1,0:T(8,128)S(1)} %get-tuple-element.13.moment, f32[512,512]{1,0:T(8,128)S(1)} %get-tuple-element.14.left_stat, ...), custom_call_target="tpu_custom_call" | custom-call | flops 134217728 | bytes 3670016 | tf_op jit(solution)/shard_map/pallas_call | solution.py:426

commit v3 on v1

--- a/solution.py
+++ b/solution.py
@@ -23,14 +23,12 @@
     )
 
 
-def widen(source, wide):
-    depth, fan = source.shape[:2]
-    step = min(fan, 32)
+def widen(source, wide, start, row):
+    fan, depth = source.shape[:2]
     for i in range(depth):
-        for j in range(0, fan, step):
-            part = source[i, j : j + step].astype(jnp.float32)
-            start = (i * fan + j) * SUBLANES
-            wide[start : start + step * SUBLANES, :] = part.reshape(step * SUBLANES, LANES)
+        part = source[pl.ds(start, row), i].astype(jnp.float32)
+        first = (i * fan + start) * SUBLANES
+        wide[pl.ds(first, row * SUBLANES), :] = part.reshape(row * SUBLANES, LANES)
 
 
 def alternate(count):
@@ -58,9 +56,11 @@
     wide,
     sent,
     relay,
+    staged,
     landed,
     sent_back,
     relay_back,
+    staged_back,
     block,
     norms,
     norms_z,
@@ -74,7 +74,7 @@
     norm_send,
     norm_recv,
 ):
-    fan = relay.shape[0]
+    fan = relay.shape[1]
     row = fan // across
     blocks = depth * fan
     side = block.shape[0]
@@ -126,48 +126,47 @@
             target[i : i + step] = part.reshape(step, SUBLANES, LANES).astype(jnp.bfloat16)
 
     def chunk_of(k):
-        return ((x + k) % across) * row
+        return pl.multiple_of(((x + k) % across) * row, row)
 
     def send_z(k, source, through, way):
         start = chunk_of(k)
-
         for j in alternate(depth):
             to = (g + j) % depth
             pltpu.make_async_remote_copy(
                 src_ref=source.at[pl.ds(to * fan + start, row)],
-                dst_ref=through.at[pl.ds(start, row), g],
+                dst_ref=through.at[g, pl.ds(start, row)],
                 send_sem=z_send.at[way],
                 recv_sem=z_recv.at[way, k],
                 device_id=(to, f),
                 device_id_type=MESH,
             ).start()
-        pltpu.make_async_copy(
-            source.at[pl.ds(g * fan + start, row)],
-            through.at[pl.ds(start, row), g],
-            z_recv.at[way, k],
-        ).start()
-
-    def send_f(k, through, target, way):
+
+    def send_f(k, source, through, turned, target, way):
         start = chunk_of(k)
-        arrived = through.at[pl.ds(start, row)]
+        arrived = through.at[pl.ds(0, depth - 1), pl.ds(start, row)]
         pltpu.make_async_copy(arrived, arrived, z_recv.at[way, k]).wait()
+        through[g, pl.ds(start, row)] = source[pl.ds(g * fan + start, row)]
+        for i in range(depth):
+            turned[pl.ds(start, row), i] = through[i, pl.ds(start, row)]
         place = f % row
-
         for j in alternate(row) + ([] if k == 0 else [0]):
             to = start + (place + j) % row
             pltpu.make_async_remote_copy(
-                src_ref=through.at[to],
-                dst_ref=target.at[:, f],
+                src_ref=turned.at[to],
+                dst_ref=target.at[f],
                 send_sem=f_send.at[way],
-                recv_sem=f_recv.at[way],
+                recv_sem=f_recv.at[way, k],
                 device_id=(g, to),
                 device_id_type=MESH,
             ).start()
+
+    def wait_chunk(k, turned, target, way):
+        start = pl.multiple_of(((x + across - k) % across) * row, row)
+        arrived = target.at[pl.ds(0, row - (k == 0))]
+        pltpu.make_async_copy(arrived, arrived, f_recv.at[way, k]).wait()
         if k == 0:
-            pltpu.make_async_copy(through.at[f], target.at[:, f], f_recv.at[way]).start()
-
-    def wait_all(target, way):
-        pltpu.make_async_copy(target, target, f_recv.at[way]).wait()
+            target[f] = turned[f]
+        return start
 
     def wait_sent(source, through, way):
         part = source.at[pl.ds(0, (depth - 1) * fan)]
@@ -184,7 +183,7 @@
         wide[pl.ds(c + 1, blocks, stride=SUBLANES), :] = pair[:, LANES:]
     narrow(sent)
     pl.semaphore_wait(barrier, depth - 1 + fan - 1)
-    for k in chunks[:2]:
+    for k in chunks:
         send_z(k, sent, relay, 0)
 
     loads[2].wait()
@@ -199,11 +198,6 @@
         squares = jnp.sum(direction * direction, axis=1, keepdims=True)
         share = share + jnp.sum(holds[i : i + tall, :] * squares, axis=0, keepdims=True)
     norms[...] = share
-    for i, k in enumerate(chunks):
-        send_f(k, relay, landed, 0)
-        if i + 2 < across:
-            send_z(chunks[i + 2], sent, relay, 0)
-
     def norm_z(j, carry):
         pltpu.make_async_remote_copy(
             src_ref=norms,
@@ -216,9 +210,6 @@
         return carry
 
     lax.fori_loop(1, depth, norm_z, 0)
-    pltpu.make_async_copy(norms, norms_z.at[g], norm_recv.at[0]).start()
-    pltpu.make_async_copy(norms_z, norms_z, norm_recv.at[0]).wait()
-    norms_z_sum[...] = jnp.sum(norms_z[...], axis=0)
 
     def norm_f(j, carry):
         pltpu.make_async_remote_copy(
@@ -231,22 +222,35 @@
         ).start()
         return carry
 
-    lax.fori_loop(1, fan, norm_f, 0)
-    pltpu.make_async_copy(norms_z_sum, norms_f.at[f], norm_recv.at[1]).start()
-
-    wait_all(landed, 0)
-    widen(landed, wide)
-    for c in range(pieces):
-        block[:, c * LANES : (c + 1) * LANES] = wide[pl.ds(c, side, stride=pieces), :].astype(
-            jnp.bfloat16
-        )
+    for i, k in enumerate(chunks):
+        send_f(k, sent, relay, staged, landed, 0)
+        if i == min(1, across - 1):
+            arrived = norms_z.at[pl.ds(0, depth - 1)]
+            pltpu.make_async_copy(arrived, arrived, norm_recv.at[0]).wait()
+            norms_z[g] = norms[...]
+            norms_z_sum[...] = jnp.sum(norms_z[...], axis=0)
+            lax.fori_loop(1, fan, norm_f, 0)
+
+    for k in chunks:
+        start = wait_chunk(k, staged, landed, 0)
+        widen(landed, wide, start, row)
+        tall = row * SUBLANES // pieces
+        for i in range(depth):
+            first = (i * fan + start) * SUBLANES
+            rows = pl.ds(pl.multiple_of((i * fan + start) * SUBLANES // pieces, tall), tall)
+            for c in range(pieces):
+                block[rows, c * LANES : (c + 1) * LANES] = wide[
+                    pl.ds(first + c, tall, stride=pieces), :
+                ].astype(jnp.bfloat16)
     loads[3].wait()
     loads[4].wait()
     half = matmul(left_root[...], block[...]).astype(jnp.bfloat16)
     full = matmul(half, right_root[...])
     precon_sq = jnp.sum(full * full, keepdims=True)
     precon = full.astype(jnp.bfloat16).astype(jnp.float32)
-    pltpu.make_async_copy(norms_f, norms_f, norm_recv.at[1]).wait()
+    arrived = norms_f.at[pl.ds(0, fan - 1)]
+    pltpu.make_async_copy(arrived, arrived, norm_recv.at[1]).wait()
+    norms_f[f] = norms_z_sum[...]
     totals = jnp.sum(norms_f[...], axis=0)
     lane = lax.broadcasted_iota(jnp.int32, (1, blocks), 1)
     adam_sq = jnp.sum(jnp.where(lane == me, totals, 0.0), keepdims=True)
@@ -256,7 +260,7 @@
         wide[pl.ds(c, side, stride=pieces), :] = scaled[:, c * LANES : (c + 1) * LANES]
     narrow(sent_back)
 
-    for k in chunks[:2]:
+    for k in chunks:
         send_z(k, sent_back, relay_back, 1)
     loads[5].wait()
     left = matmul(block[...], block[...], 1, 1)
@@ -264,13 +268,12 @@
     loads[6].wait()
     right = matmul(block[...], block[...], 0, 0)
     right_stat[...] = STAT_DECAY * right_stat[...] + (1.0 - STAT_DECAY) * right / side
-    for i, k in enumerate(chunks):
-        send_f(k, relay_back, landed_back, 1)
-        if i + 2 < across:
-            send_z(chunks[i + 2], sent_back, relay_back, 1)
-    wait_all(landed_back, 1)
-    wait_sent(sent, relay, 0)
-    wait_sent(sent_back, relay_back, 1)
+    for k in chunks:
+        send_f(k, sent_back, relay_back, staged_back, landed_back, 1)
+    for k in chunks:
+        wait_chunk(k, staged_back, landed_back, 1)
+    wait_sent(sent, staged, 0)
+    wait_sent(sent_back, staged_back, 1)
     part = norms_z.at[pl.ds(0, depth - 1)]
     pltpu.make_async_copy(part, part, norm_send.at[0]).wait()
     part = norms_f.at[pl.ds(0, fan - 1)]
@@ -301,7 +304,7 @@
     ]
     for store in stores:
         store.start()
-    widen(landed, wide)
+    widen(landed, wide, 0, landed.shape[0])
     load.wait()
     blocks = update.shape[0]
     which = lax.broadcasted_iota(jnp.int32, (blocks, blocks), 0)
@@ -335,7 +338,7 @@
     landed, moment_new, left_new, right_new = pl.pallas_call(
         functools.partial(exchange, depth, across),
         out_shape=(
-            jax.ShapeDtypeStruct((depth, fan, *tile), bf16),
+            jax.ShapeDtypeStruct((fan, depth, *tile), bf16),
             entry_shapes,
             stat_shapes,
             stat_shapes,
@@ -349,9 +352,11 @@
             pltpu.VMEM((side, side), bf16),
             pltpu.VMEM((blocks * SUBLANES, LANES), f32),
             pltpu.VMEM((blocks, *tile), bf16),
+            pltpu.VMEM((depth, fan, *tile), bf16),
             pltpu.VMEM((fan, depth, *tile), bf16),
+            pltpu.VMEM((fan, depth, *tile), bf16),
+            pltpu.VMEM((blocks, *tile), bf16),
             pltpu.VMEM((depth, fan, *tile), bf16),
-            pltpu.VMEM((blocks, *tile), bf16),
             pltpu.VMEM((fan, depth, *tile), bf16),
             pltpu.VMEM((side, side), bf16),
             pltpu.VMEM((1, blocks), f32),
@@ -362,7 +367,7 @@
             pltpu.SemaphoreType.DMA((2,)),
             pltpu.SemaphoreType.DMA((2, across)),
             pltpu.SemaphoreType.DMA((2,)),
-            pltpu.SemaphoreType.DMA((2,)),
+            pltpu.SemaphoreType.DMA((2, across)),
             pltpu.SemaphoreType.DMA((2,)),
             pltpu.SemaphoreType.DMA((2,)),
         ],

time: 55.4 us -> 52.9 us (0.955)
  Pallas kernels: 54.7 us -> 52.2 us
    pallas_call x1, Pallas kernels: 52.8 us -> 50.3 us  [shards(): pl.pallas_call(functools.partial(exchange, depth, across), out_shape=(jax...]
where the time goes in v3:
time: 52.9 us; the launch traced here: 52.8 us
  Pallas kernels  52.2 us (99%)
  between operations  0.64 us (1%)
    pallas_call x1, Pallas kernels, shards(): pl.pallas_call(functools.partial(exchange, depth, across), out_shape=(jax...  50.3 us
    pallas_call x1, Pallas kernels, shards(): pl.pallas_call(write, out_shape=(jax.ShapeDtypeStruct((blocks, entries),...  1.89 us

profile of v3, /device:TPU:1, one launch (start us, length us, event | category | flops | bytes accessed | tf_op | source)
XLA Modules:
  0.0 52.8 jit_solution(9205719775621056460)
XLA Ops:
  0.6 50.3 %shard_map.102 = (bf16[32,8,8,128]{3,2,1,0:T(8,128)(2,1)S(1)}, f32[256,1024]{1,0:T(8,128)S(1)}, f32[512,512]{1,0:T(8,128)S(1)}, f32[512,512]{1,0:T(8,128)S(1)}) custom-call(bf16[256,1024]{1,0:T(8,128)(2,1)} %grad_hbm.1, f32[256,1024]{1,0:T(8,128)} %moment_hbm.1, s32[1,256]{1,0:T(1,128)} %bitcast.11, f32[512,512]{1,0:T(8,128)} %bitcast.7, ...), custom_call_target="tpu_custom_call" | custom-call | flops 1207959552 | bytes 4718592 | tf_op jit(solution)/shard_map/pallas_call | solution.py:338
  50.9 1.9 %shard_map.103 = (bf16[256,1024]{1,0:T(8,128)(2,1)}, f32[256,1024]{1,0:T(8,128)}, f32[512,512]{1,0:T(8,128)}, f32[512,512]{1,0:T(8,128)}) custom-call(bf16[32,8,8,128]{3,2,1,0:T(8,128)(2,1)S(1)} %get-tuple-element.12.landed, f32[256,1024]{1,0:T(8,128)S(1)} %get-tuple-element.13.moment, f32[512,512]{1,0:T(8,128)S(1)} %get-tuple-element.14.left_stat, ...), custom_call_target="tpu_custom_call" | custom-call | flops 134217728 | bytes 3670016 | tf_op jit(solution)/shard_map/pallas_call | solution.py:396

commit v4 on v1

v4 whole, which is shorter than its diff:
```python
import functools

import jax
import jax.numpy as jnp
from jax import lax
from jax.experimental import pallas as pl
from jax.experimental.pallas import tpu as pltpu
from jax.sharding import PartitionSpec as P

MOMENT_DECAY = 0.95
STAT_DECAY = 0.9
ADAM_EPS = 1e-08
PRECON_EPS = 1e-06

LANES = 128
SUBLANES = 8
MESH = pl.DeviceIdType.MESH


def matmul(a, b, a_dim=1, b_dim=0):
    return lax.dot_general(
        a, b, (((a_dim,), (b_dim,)), ((), ())), preferred_element_type=jnp.float32
    )


def alternate(count):
    return sorted(range(1, count), key=lambda k: (-min(k, count - k), k))


def exchange(
    depth,
    across,
    grad_hbm,
    moment_hbm,
    order_hbm,
    left_stat_hbm,
    right_stat_hbm,
    left_root_hbm,
    right_root_hbm,
    wide_back,
    totals,
    moment,
    left_stat,
    right_stat,
    order,
    grad,
    left_root,
    right_root,
    wide,
    sent,
    via_z,
    turned_z,
    landed_xy,
    turned_xy,
    via_xy,
    turned_back,
    landed_z,
    block,
    norms,
    norms_z,
    norms_z_sum,
    norms_f,
    load_sem,
    z_send,
    z_recv,
    xy_send,
    xy_recv,
    norm_send,
    norm_recv,
):
    plane = via_xy.shape[1]
    deep = plane // across
    fan = plane * 2
    blocks = depth * fan
    side = block.shape[0]
    pieces = side // LANES
    g = lax.axis_index("group")
    f = lax.axis_index("fsdp")
    xy = f // 2
    core = f % 2
    x = xy // deep
    y = xy % deep
    me = g * fan + f

    loads = [
        pltpu.make_async_copy(source, target, load_sem.at[i])
        for i, (source, target) in enumerate(
            (
                (order_hbm, order),
                (grad_hbm, grad),
                (moment_hbm, moment),
                (left_root_hbm, left_root),
                (right_root_hbm, right_root),
                (left_stat_hbm, left_stat),
                (right_stat_hbm, right_stat),
            )
        )
    ]
    for load in loads:
        load.start()

    barrier = pltpu.get_barrier_semaphore()

    def greet_z(k, carry):
        to = lax.rem(g + k, depth)
        pl.semaphore_signal(barrier, inc=1, device_id=(to, f), device_id_type=MESH)
        return carry

    def greet_f(k, carry):
        to = lax.rem(f + k, fan)
        pl.semaphore_signal(barrier, inc=1, device_id=(g, to), device_id_type=MESH)
        return carry

    lax.fori_loop(1, depth, greet_z, 0)
    lax.fori_loop(1, fan, greet_f, 0)

    loads[0].wait()
    which = lax.broadcasted_iota(jnp.int32, (blocks, blocks), 0)
    holds = jnp.where(which == order[...], 1.0, 0.0)
    slots_half = holds.T.astype(jnp.bfloat16)

    def narrow():
        rows = fan * SUBLANES
        for i in range(depth):
            part = wide[i * rows : (i + 1) * rows, :].reshape(plane, 2, SUBLANES, LANES)
            for c in range(2):
                sent[way, c, i] = part[:, c].astype(jnp.bfloat16)

    def widen(target, i, c, part):
        part = part.astype(jnp.float32)
        first = pl.multiple_of((i * fan + c) * SUBLANES, SUBLANES)
        for j in range(plane):
            target[pl.ds(first + j * 2 * SUBLANES, SUBLANES), :] = part[j]

    near_first = sorted(
        range(1, plane),
        key=lambda j: (
            min(j // deep, across - j // deep) + min(j % deep, deep - j % deep),
            j,
        ),
    )

    def place(j):
        tx = lax.rem(x + j // deep, across)
        ty = lax.rem(y + j % deep, deep)
        return tx * deep + ty

    def send_z(source, target, half):
        for j in alternate(depth):
            to = lax.rem(g + j, depth)
            pltpu.make_async_remote_copy(
                src_ref=source(to),
                dst_ref=target.at[way, g],
                send_sem=z_send.at[way, half],
                recv_sem=z_recv.at[way, half],
                device_id=(to, f),
                device_id_type=MESH,
            ).start()

    def send_xy(source, target, half, to_core, places):
        for j in places:
            to = place(j)
            pltpu.make_async_remote_copy(
                src_ref=source.at[way, to],
                dst_ref=target.at[way, xy],
                send_sem=xy_send.at[way, half],
                recv_sem=xy_recv.at[way, half],
                device_id=(g, to * 2 + to_core),
                device_id_type=MESH,
            ).start()

    def wait(part, sem):
        pltpu.make_async_copy(part, part, sem).wait()

    def begin():
        send_z(lambda to: sent.at[way, core, to], via_z, 0)
        via_z[way, g] = sent[way, core, g]
        for i in range(depth):
            turned_xy[way, :, i] = sent[way, 1 - core, i]
        send_xy(turned_xy, via_xy, 1, 1 - core, near_first[::-1] + [0])

    def go_on_z():
        wait(via_xy.at[way], xy_recv.at[way, 1])
        for i in range(depth):
            turned_back[way, i] = via_xy[way, :, i]
        send_z(lambda to: turned_back.at[way, to], landed_z, 1)
        landed_z[way, g] = turned_back[way, g]

    def go_on_xy():
        wait(via_z.at[way, pl.ds(0, depth - 1)], z_recv.at[way, 0])
        for i in range(depth):
            turned_z[way, :, i] = via_z[way, i]
        send_xy(turned_z, landed_xy, 0, core, near_first[::-1])
        landed_xy[way, xy] = turned_z[way, xy]

    def end(target):
        wait(landed_xy.at[way, pl.ds(0, plane - 1)], xy_recv.at[way, 0])

        def from_xy(i, carry):
            widen(target, i, core, landed_xy[way, :, i])
            return carry

        lax.fori_loop(0, depth, from_xy, 0)
        wait(landed_z.at[way, pl.ds(0, depth - 1)], z_recv.at[way, 1])

        def from_z(i, carry):
            widen(target, i, 1 - core, landed_z[way, i])
            return carry

        lax.fori_loop(0, depth, from_z, 0)

    way = 0
    loads[1].wait()
    for c in range(0, SUBLANES, 2):
        pair = matmul(slots_half, grad[:, c * LANES : (c + 2) * LANES])
        wide[pl.ds(c, blocks, stride=SUBLANES), :] = pair[:, :LANES]
        wide[pl.ds(c + 1, blocks, stride=SUBLANES), :] = pair[:, LANES:]
    narrow()
    pl.semaphore_wait(barrier, depth - 1 + fan - 1)
    begin()

    loads[2].wait()
    tall = min(blocks, 32)
    share = jnp.zeros((1, blocks), jnp.float32)
    for i in range(0, blocks, tall):
        rows = pl.ds(i, tall)
        gradient = grad[rows, :].astype(jnp.float32)
        second = MOMENT_DECAY * moment[rows, :] + (1.0 - MOMENT_DECAY) * gradient * gradient
        moment[rows, :] = second
        direction = gradient / (jnp.sqrt(second) + ADAM_EPS)
        squares = jnp.sum(direction * direction, axis=1, keepdims=True)
        share = share + jnp.sum(holds[i : i + tall, :] * squares, axis=0, keepdims=True)
    norms[0:1, :] = share
    go_on_z()
    go_on_xy()

    end(wide)
    for c in range(pieces):
        block[:, c * LANES : (c + 1) * LANES] = wide[pl.ds(c, side, stride=pieces), :].astype(
            jnp.bfloat16
        )
    loads[3].wait()
    loads[4].wait()
    half = matmul(left_root[...], block[...]).astype(jnp.bfloat16)
    full = matmul(half, right_root[...])
    for c in range(pieces):
        wide[pl.ds(c, side, stride=pieces), :] = full[:, c * LANES : (c + 1) * LANES]

    way = 1
    narrow()
    begin()

    lane = lax.broadcasted_iota(jnp.int32, (1, blocks), 1)
    precon_sq = jnp.sum(full * full, keepdims=True)
    norms[1:2, :] = jnp.where(lane == me, precon_sq, 0.0)

    def norm_z(j, carry):
        pltpu.make_async_remote_copy(
            src_ref=norms,
            dst_ref=norms_z.at[g],
            send_sem=norm_send.at[0],
            recv_sem=norm_recv.at[0],
            device_id=((g + j) % depth, f),
            device_id_type=MESH,
        ).start()
        return carry

    def norm_f(j, carry):
        pltpu.make_async_remote_copy(
            src_ref=norms_z_sum,
            dst_ref=norms_f.at[f],
            send_sem=norm_send.at[1],
            recv_sem=norm_recv.at[1],
            device_id=(g, (f + j) % fan),
            device_id_type=MESH,
        ).start()
        return carry

    lax.fori_loop(1, depth, norm_z, 0)

    loads[5].wait()
    left = matmul(block[...], block[...], 1, 1)
    left_stat[...] = STAT_DECAY * left_stat[...] + (1.0 - STAT_DECAY) * left / side
    loads[6].wait()
    right = matmul(block[...], block[...], 0, 0)
    right_stat[...] = STAT_DECAY * right_stat[...] + (1.0 - STAT_DECAY) * right / side
    go_on_z()
    arrived = norms_z.at[pl.ds(0, depth - 1)]
    pltpu.make_async_copy(arrived, arrived, norm_recv.at[0]).wait()
    norms_z[g] = norms[...]
    norms_z_sum[...] = jnp.sum(norms_z[...], axis=0)
    lax.fori_loop(1, fan, norm_f, 0)
    go_on_xy()
    end(wide_back)
    arrived = norms_f.at[pl.ds(0, fan - 1)]
    pltpu.make_async_copy(arrived, arrived, norm_recv.at[1]).wait()
    norms_f[f] = norms_z_sum[...]
    totals[...] = jnp.sum(norms_f[...], axis=0)

    for way in range(2):
        wait(via_z.at[way, pl.ds(0, depth - 1)], z_send.at[way, 0])
        wait(landed_z.at[way, pl.ds(0, depth - 1)], z_send.at[way, 1])
        wait(landed_xy.at[way, pl.ds(0, plane - 1)], xy_send.at[way, 0])
        wait(via_xy.at[way], xy_send.at[way, 1])
    part = norms_z.at[pl.ds(0, depth - 1)]
    pltpu.make_async_copy(part, part, norm_send.at[0]).wait()
    part = norms_f.at[pl.ds(0, fan - 1)]
    pltpu.make_async_copy(part, part, norm_send.at[1]).wait()


def write(
    wide,
    totals,
    moment,
    left_stat,
    right_stat,
    order_hbm,
    update_hbm,
    moment_hbm,
    left_hbm,
    right_hbm,
    order,
    update,
    sems,
):
    load = pltpu.make_async_copy(order_hbm, order, sems.at[0])
    load.start()
    stores = [
        pltpu.make_async_copy(moment, moment_hbm, sems.at[1]),
        pltpu.make_async_copy(left_stat, left_hbm, sems.at[2]),
        pltpu.make_async_copy(right_stat, right_hbm, sems.at[3]),
    ]
    for store in stores:
        store.start()
    load.wait()
    blocks = update.shape[0]
    which = lax.broadcasted_iota(jnp.int32, (blocks, blocks), 0)
    holds = jnp.where(which == order[...], 1.0, 0.0)
    scale = jnp.sqrt(totals[0:1, :]) / (jnp.sqrt(totals[1:2, :]) + PRECON_EPS)
    scale = jnp.sum(holds * scale, axis=1, keepdims=True)
    holds = holds.astype(jnp.bfloat16)
    for c in range(0, SUBLANES, 2):
        pair = jnp.concatenate(
            [wide[pl.ds(c + i, blocks, stride=SUBLANES), :] for i in range(2)], axis=1
        ).astype(jnp.bfloat16)
        columns = pl.ds(c * LANES, 2 * LANES)
        update[:, columns] = (matmul(holds, pair) * scale).astype(jnp.bfloat16)
        stores.append(
            pltpu.make_async_copy(update.at[:, columns], update_hbm.at[:, columns], sems.at[4 + c // 2])
        )
        stores[-1].start()
    for store in stores:
        store.wait()


def shards(across, grad, moment, order, left_stat, right_stat, left_root, right_root):
    depth = lax.axis_size("group")
    fan = lax.axis_size("fsdp")
    plane = fan // 2
    blocks, entries = grad.shape
    side = left_stat.shape[-1]
    f32, bf16 = jnp.float32, jnp.bfloat16
    tile = (SUBLANES, LANES)
    hbm = pl.BlockSpec(memory_space=pltpu.HBM)
    vmem = pl.BlockSpec(memory_space=pltpu.VMEM)
    order = order.reshape(1, blocks)
    entry_shapes = jax.ShapeDtypeStruct((blocks, entries), f32)
    stat_shapes = jax.ShapeDtypeStruct((side, side), f32)
    wide, totals, moment_new, left_new, right_new = pl.pallas_call(
        functools.partial(exchange, depth, across),
        out_shape=(
            jax.ShapeDtypeStruct((blocks * SUBLANES, LANES), f32),
            jax.ShapeDtypeStruct((2, blocks), f32),
            entry_shapes,
            stat_shapes,
            stat_shapes,
        ),
        in_specs=[hbm] * 7,
        out_specs=(vmem,) * 5,
        scratch_shapes=[
            pltpu.VMEM((1, blocks), jnp.int32),
            pltpu.VMEM((blocks, entries), bf16),
            pltpu.VMEM((side, side), bf16),
            pltpu.VMEM((side, side), bf16),
            pltpu.VMEM((blocks * SUBLANES, LANES), f32),
            pltpu.VMEM((2, 2, depth, plane, *tile), bf16),
            pltpu.VMEM((2, depth, plane, *tile), bf16),
            pltpu.VMEM((2, plane, depth, *tile), bf16),
            pltpu.VMEM((2, plane, depth, *tile), bf16),
            pltpu.VMEM((2, plane, depth, *tile), bf16),
            pltpu.VMEM((2, plane, depth, *tile), bf16),
            pltpu.VMEM((2, depth, plane, *tile), bf16),
            pltpu.VMEM((2, depth, plane, *tile), bf16),
            pltpu.VMEM((side, side), bf16),
            pltpu.VMEM((2, blocks), f32),
            pltpu.VMEM((depth, 2, blocks), f32),
            pltpu.VMEM((2, blocks), f32),
            pltpu.VMEM((fan, 2, blocks), f32),
            pltpu.SemaphoreType.DMA((7,)),
            pltpu.SemaphoreType.DMA((2, 2)),
            pltpu.SemaphoreType.DMA((2, 2)),
            pltpu.SemaphoreType.DMA((2, 2)),
            pltpu.SemaphoreType.DMA((2, 2)),
            pltpu.SemaphoreType.DMA((2,)),
            pltpu.SemaphoreType.DMA((2,)),
        ],
        compiler_params=pltpu.CompilerParams(
            collective_id=0, has_side_effects=True, vmem_limit_bytes=40 * 1024 * 1024
        ),
        cost_estimate=pl.CostEstimate(
            flops=8 * side**3 + 2 * blocks * blocks * entries,
            bytes_accessed=6 * blocks * entries + 12 * side * side,
            transcendentals=2 * blocks * entries,
        ),
    )(
        *(
            pltpu.with_memory_space_constraint(operand, pltpu.HBM)
            for operand in (
                grad,
                moment,
                order,
                left_stat[0],
                right_stat[0],
                left_root[0],
                right_root[0],
            )
        )
    )
    update, moment_new, left_new, right_new = pl.pallas_call(
        write,
        out_shape=(
            jax.ShapeDtypeStruct((blocks, entries), bf16),
            entry_shapes,
            stat_shapes,
            stat_shapes,
        ),
        in_specs=[vmem] * 5 + [hbm],
        out_specs=(hbm,) * 4,
        scratch_shapes=[
            pltpu.VMEM((1, blocks), jnp.int32),
            pltpu.VMEM((blocks, entries), bf16),
            pltpu.SemaphoreType.DMA((8,)),
        ],
        compiler_params=pltpu.CompilerParams(vmem_limit_bytes=40 * 1024 * 1024),
        cost_estimate=pl.CostEstimate(
            flops=2 * blocks * blocks * entries,
            bytes_accessed=6 * blocks * entries + 8 * side * side,
            transcendentals=0,
        ),
    )(
        wide,
        totals,
        moment_new,
        left_new,
        right_new,
        pltpu.with_memory_space_constraint(order, pltpu.HBM),
    )
    return (update, moment_new, left_new[None], right_new[None])


def solution(mesh):
    across = 4 if mesh.shape["fsdp"] == 32 else 2
    placed = (
        P(None, ("group", "fsdp")),
        P(None, ("group", "fsdp")),
        P(),
        P(("group", "fsdp"), None, None),
        P(("group", "fsdp"), None, None),
        P(("group", "fsdp"), None, None),
        P(("group", "fsdp"), None, None),
    )
    return jax.shard_map(
        functools.partial(shards, across),
        mesh=mesh,
        in_specs=placed,
        out_specs=(
            P(None, ("group", "fsdp")),
            P(None, ("group", "fsdp")),
            P(("group", "fsdp"), None, None),
            P(("group", "fsdp"), None, None),
        ),
        check_vma=False,
    )
```

time: 55.4 us -> 43.3 us (0.78)
  Pallas kernels: 54.7 us -> 42.5 us
    pallas_call x1, Pallas kernels: 52.8 us -> 40.6 us  [shards(): pl.pallas_call(functools.partial(exchange, depth, across), out_shape=(jax...]
where the time goes in v4:
time: 43.3 us; the launch traced here: 43.1 us
  Pallas kernels  42.5 us (98%)
  between operations  0.64 us (1%)
    pallas_call x1, Pallas kernels, shards(): pl.pallas_call(functools.partial(exchange, depth, across), out_shape=(jax...  40.6 us
    pallas_call x1, Pallas kernels, shards(): pl.pallas_call(write, out_shape=(jax.ShapeDtypeStruct((blocks, entries),...  1.89 us

profile of v4, /device:TPU:1, one launch (start us, length us, event | category | flops | bytes accessed | tf_op | source)
XLA Modules:
  0.0 43.1 jit_solution(476221943178527178)
XLA Ops:
  0.6 40.6 %shard_map.102 = (f32[2048,128]{1,0:T(8,128)S(1)}, f32[2,256]{1,0:T(2,128)S(1)}, f32[256,1024]{1,0:T(8,128)S(1)}, f32[512,512]{1,0:T(8,128)S(1)}, f32[512,512]{1,0:T(8,128)S(1)}) custom-call(bf16[256,1024]{1,0:T(8,128)(2,1)} %grad_hbm.1, f32[256,1024]{1,0:T(8,128)} %moment_hbm.1, s32[1,256]{1,0:T(1,128)} %bitcast.11, f32[512,512]{1,0:T(8,128)} %bitcast.7, ...), custom_call_target="tpu_custom_call" | custom-call | flops 1207959552 | bytes 4718592 | tf_op jit(solution)/shard_map/pallas_call | solution.py:369
  41.3 1.9 %shard_map.103 = (bf16[256,1024]{1,0:T(8,128)(2,1)}, f32[256,1024]{1,0:T(8,128)}, f32[512,512]{1,0:T(8,128)}, f32[512,512]{1,0:T(8,128)}) custom-call(f32[2048,128]{1,0:T(8,128)S(1)} %get-tuple-element.13.wide, f32[2,256]{1,0:T(2,128)S(1)} %get-tuple-element.14.totals, f32[256,1024]{1,0:T(8,128)S(1)} %get-tuple-element.15.moment, ...), custom_call_target="tpu_custom_call" | custom-call | flops 134217728 | bytes 3670016 | tf_op jit(solution)/shard_map/pallas_call | solution.py:429

commit v5 on v4

--- a/solution.py
+++ b/solution.py
@@ -39,6 +39,7 @@
     right_root_hbm,
     wide_back,
     totals,
+    holds_half,
     moment,
     left_stat,
     right_stat,
@@ -57,9 +58,11 @@
     landed_z,
     block,
     norms,
+    norms_core,
+    norms_core_sum,
     norms_z,
     norms_z_sum,
-    norms_f,
+    norms_xy,
     load_sem,
     z_send,
     z_recv,
@@ -117,14 +120,12 @@
     loads[0].wait()
     which = lax.broadcasted_iota(jnp.int32, (blocks, blocks), 0)
     holds = jnp.where(which == order[...], 1.0, 0.0)
+    holds_half[...] = holds.astype(jnp.bfloat16)
     slots_half = holds.T.astype(jnp.bfloat16)
 
-    def narrow():
-        rows = fan * SUBLANES
-        for i in range(depth):
-            part = wide[i * rows : (i + 1) * rows, :].reshape(plane, 2, SUBLANES, LANES)
-            for c in range(2):
-                sent[way, c, i] = part[:, c].astype(jnp.bfloat16)
+    def tile(i, j, c):
+        first = pl.multiple_of((i * fan + j * 2 + c) * SUBLANES, SUBLANES)
+        return wide[pl.ds(first, SUBLANES), :].astype(jnp.bfloat16)
 
     def widen(target, i, c, part):
         part = part.astype(jnp.float32)
@@ -145,17 +146,16 @@
         ty = lax.rem(y + j % deep, deep)
         return tx * deep + ty
 
-    def send_z(source, target, half):
-        for j in alternate(depth):
-            to = lax.rem(g + j, depth)
-            pltpu.make_async_remote_copy(
-                src_ref=source(to),
-                dst_ref=target.at[way, g],
-                send_sem=z_send.at[way, half],
-                recv_sem=z_recv.at[way, half],
-                device_id=(to, f),
-                device_id_type=MESH,
-            ).start()
+    def send_z(j, source, target, half):
+        to = lax.rem(g + j, depth)
+        pltpu.make_async_remote_copy(
+            src_ref=source.at[way, to],
+            dst_ref=target.at[way, g],
+            send_sem=z_send.at[way, half],
+            recv_sem=z_recv.at[way, half],
+            device_id=(to, f),
+            device_id_type=MESH,
+        ).start()
 
     def send_xy(source, target, half, to_core, places):
         for j in places:
@@ -173,17 +173,28 @@
         pltpu.make_async_copy(part, part, sem).wait()
 
     def begin():
-        send_z(lambda to: sent.at[way, core, to], via_z, 0)
-        via_z[way, g] = sent[way, core, g]
-        for i in range(depth):
-            turned_xy[way, :, i] = sent[way, 1 - core, i]
+        for k in alternate(depth):
+            to = lax.rem(g + k, depth)
+            for j in range(plane):
+                sent[way, to, j] = tile(to, j, core)
+            send_z(k, sent, via_z, 0)
+
+        def fill(i, carry):
+            for j in range(plane):
+                turned_xy[way, j, i] = tile(i, j, 1 - core)
+            return carry
+
+        lax.fori_loop(0, depth, fill, 0)
         send_xy(turned_xy, via_xy, 1, 1 - core, near_first[::-1] + [0])
+        for j in range(plane):
+            via_z[way, g, j] = tile(g, j, core)
 
     def go_on_z():
         wait(via_xy.at[way], xy_recv.at[way, 1])
         for i in range(depth):
             turned_back[way, i] = via_xy[way, :, i]
-        send_z(lambda to: turned_back.at[way, to], landed_z, 1)
+        for k in alternate(depth):
+            send_z(k, turned_back, landed_z, 1)
         landed_z[way, g] = turned_back[way, g]
 
     def go_on_xy():
@@ -215,7 +226,6 @@
         pair = matmul(slots_half, grad[:, c * LANES : (c + 2) * LANES])
         wide[pl.ds(c, blocks, stride=SUBLANES), :] = pair[:, :LANES]
         wide[pl.ds(c + 1, blocks, stride=SUBLANES), :] = pair[:, LANES:]
-    narrow()
     pl.semaphore_wait(barrier, depth - 1 + fan - 1)
     begin()
 
@@ -247,106 +257,102 @@
         wide[pl.ds(c, side, stride=pieces), :] = full[:, c * LANES : (c + 1) * LANES]
 
     way = 1
-    narrow()
     begin()
 
     lane = lax.broadcasted_iota(jnp.int32, (1, blocks), 1)
     precon_sq = jnp.sum(full * full, keepdims=True)
     norms[1:2, :] = jnp.where(lane == me, precon_sq, 0.0)
 
+    swap = pltpu.make_async_remote_copy(
+        src_ref=norms,
+        dst_ref=norms_core,
+        send_sem=norm_send.at[0],
+        recv_sem=norm_recv.at[0],
+        device_id=(g, xy * 2 + 1 - core),
+        device_id_type=MESH,
+    )
+    swap.start()
+
     def norm_z(j, carry):
         pltpu.make_async_remote_copy(
-            src_ref=norms,
+            src_ref=norms_core_sum,
             dst_ref=norms_z.at[g],
-            send_sem=norm_send.at[0],
-            recv_sem=norm_recv.at[0],
-            device_id=((g + j) % depth, f),
+            send_sem=norm_send.at[1],
+            recv_sem=norm_recv.at[1],
+            device_id=(lax.rem(g + j, depth), f),
             device_id_type=MESH,
         ).start()
         return carry
 
-    def norm_f(j, carry):
-        pltpu.make_async_remote_copy(
-            src_ref=norms_z_sum,
-            dst_ref=norms_f.at[f],
-            send_sem=norm_send.at[1],
-            recv_sem=norm_recv.at[1],
-            device_id=(g, (f + j) % fan),
-            device_id_type=MESH,
-        ).start()
-        return carry
-
-    lax.fori_loop(1, depth, norm_z, 0)
-
     loads[5].wait()
     left = matmul(block[...], block[...], 1, 1)
     left_stat[...] = STAT_DECAY * left_stat[...] + (1.0 - STAT_DECAY) * left / side
+    swap.wait()
+    norms_core_sum[...] = norms[...] + norms_core[...]
+    lax.fori_loop(1, depth, norm_z, 0)
     loads[6].wait()
     right = matmul(block[...], block[...], 0, 0)
     right_stat[...] = STAT_DECAY * right_stat[...] + (1.0 - STAT_DECAY) * right / side
     go_on_z()
-    arrived = norms_z.at[pl.ds(0, depth - 1)]
-    pltpu.make_async_copy(arrived, arrived, norm_recv.at[0]).wait()
-    norms_z[g] = norms[...]
+    go_on_xy()
+    wait(norms_z.at[pl.ds(0, depth - 1)], norm_recv.at[1])
+    norms_z[g] = norms_core_sum[...]
     norms_z_sum[...] = jnp.sum(norms_z[...], axis=0)
-    lax.fori_loop(1, fan, norm_f, 0)
-    go_on_xy()
+    for j in near_first:
+        pltpu.make_async_remote_copy(
+            src_ref=norms_z_sum,
+            dst_ref=norms_xy.at[xy],
+            send_sem=norm_send.at[2],
+            recv_sem=norm_recv.at[2],
+            device_id=(g, place(j) * 2 + core),
+            device_id_type=MESH,
+        ).start()
     end(wide_back)
-    arrived = norms_f.at[pl.ds(0, fan - 1)]
-    pltpu.make_async_copy(arrived, arrived, norm_recv.at[1]).wait()
-    norms_f[f] = norms_z_sum[...]
-    totals[...] = jnp.sum(norms_f[...], axis=0)
+    wait(norms_xy.at[pl.ds(0, plane - 1)], norm_recv.at[2])
+    norms_xy[xy] = norms_z_sum[...]
+    totals[...] = jnp.sum(norms_xy[...], axis=0)
 
     for way in range(2):
         wait(via_z.at[way, pl.ds(0, depth - 1)], z_send.at[way, 0])
         wait(landed_z.at[way, pl.ds(0, depth - 1)], z_send.at[way, 1])
         wait(landed_xy.at[way, pl.ds(0, plane - 1)], xy_send.at[way, 0])
         wait(via_xy.at[way], xy_send.at[way, 1])
-    part = norms_z.at[pl.ds(0, depth - 1)]
-    pltpu.make_async_copy(part, part, norm_send.at[0]).wait()
-    part = norms_f.at[pl.ds(0, fan - 1)]
-    pltpu.make_async_copy(part, part, norm_send.at[1]).wait()
+    wait(norms_z.at[pl.ds(0, depth - 1)], norm_send.at[1])
+    wait(norms_xy.at[pl.ds(0, plane - 1)], norm_send.at[2])
 
 
 def write(
     wide,
     totals,
+    holds,
     moment,
     left_stat,
     right_stat,
-    order_hbm,
     update_hbm,
     moment_hbm,
     left_hbm,
     right_hbm,
-    order,
     update,
     sems,
 ):
-    load = pltpu.make_async_copy(order_hbm, order, sems.at[0])
-    load.start()
     stores = [
-        pltpu.make_async_copy(moment, moment_hbm, sems.at[1]),
-        pltpu.make_async_copy(left_stat, left_hbm, sems.at[2]),
-        pltpu.make_async_copy(right_stat, right_hbm, sems.at[3]),
+        pltpu.make_async_copy(moment, moment_hbm, sems.at[0]),
+        pltpu.make_async_copy(left_stat, left_hbm, sems.at[1]),
+        pltpu.make_async_copy(right_stat, right_hbm, sems.at[2]),
     ]
     for store in stores:
         store.start()
-    load.wait()
     blocks = update.shape[0]
-    which = lax.broadcasted_iota(jnp.int32, (blocks, blocks), 0)
-    holds = jnp.where(which == order[...], 1.0, 0.0)
     scale = jnp.sqrt(totals[0:1, :]) / (jnp.sqrt(totals[1:2, :]) + PRECON_EPS)
-    scale = jnp.sum(holds * scale, axis=1, keepdims=True)
-    holds = holds.astype(jnp.bfloat16)
+    scale = jnp.sum(holds[...].astype(jnp.float32) * scale, axis=1, keepdims=True)
     for c in range(0, SUBLANES, 2):
         pair = jnp.concatenate(
             [wide[pl.ds(c + i, blocks, stride=SUBLANES), :] for i in range(2)], axis=1
         ).astype(jnp.bfloat16)
         columns = pl.ds(c * LANES, 2 * LANES)
-        update[:, columns] = (matmul(holds, pair) * scale).astype(jnp.bfloat16)
+        update[:, columns] = (matmul(holds[...], pair) * scale).astype(jnp.bfloat16)
         stores.append(
-            pltpu.make_async_copy(update.at[:, columns], update_hbm.at[:, columns], sems.at[4 + c // 2])
+            pltpu.make_async_copy(update.at[:, columns], update_hbm.at[:, columns], sems.at[3 + c // 2])
         )
         stores[-1].start()
     for store in stores:
@@ -366,24 +372,25 @@
     order = order.reshape(1, blocks)
     entry_shapes = jax.ShapeDtypeStruct((blocks, entries), f32)
     stat_shapes = jax.ShapeDtypeStruct((side, side), f32)
-    wide, totals, moment_new, left_new, right_new = pl.pallas_call(
+    wide, totals, holds, moment_new, left_new, right_new = pl.pallas_call(
         functools.partial(exchange, depth, across),
         out_shape=(
             jax.ShapeDtypeStruct((blocks * SUBLANES, LANES), f32),
             jax.ShapeDtypeStruct((2, blocks), f32),
+            jax.ShapeDtypeStruct((blocks, blocks), bf16),
             entry_shapes,
             stat_shapes,
             stat_shapes,
         ),
         in_specs=[hbm] * 7,
-        out_specs=(vmem,) * 5,
+        out_specs=(vmem,) * 6,
         scratch_shapes=[
             pltpu.VMEM((1, blocks), jnp.int32),
             pltpu.VMEM((blocks, entries), bf16),
             pltpu.VMEM((side, side), bf16),
             pltpu.VMEM((side, side), bf16),
             pltpu.VMEM((blocks * SUBLANES, LANES), f32),
-            pltpu.VMEM((2, 2, depth, plane, *tile), bf16),
+            pltpu.VMEM((2, depth, plane, *tile), bf16),
             pltpu.VMEM((2, depth, plane, *tile), bf16),
             pltpu.VMEM((2, plane, depth, *tile), bf16),
             pltpu.VMEM((2, plane, depth, *tile), bf16),
@@ -393,16 +400,18 @@
             pltpu.VMEM((2, depth, plane, *tile), bf16),
             pltpu.VMEM((side, side), bf16),
             pltpu.VMEM((2, blocks), f32),
+            pltpu.VMEM((2, blocks), f32),
+            pltpu.VMEM((2, blocks), f32),
             pltpu.VMEM((depth, 2, blocks), f32),
             pltpu.VMEM((2, blocks), f32),
-            pltpu.VMEM((fan, 2, blocks), f32),
+            pltpu.VMEM((plane, 2, blocks), f32),
             pltpu.SemaphoreType.DMA((7,)),
             pltpu.SemaphoreType.DMA((2, 2)),
             pltpu.SemaphoreType.DMA((2, 2)),
             pltpu.SemaphoreType.DMA((2, 2)),
             pltpu.SemaphoreType.DMA((2, 2)),
-            pltpu.SemaphoreType.DMA((2,)),
-            pltpu.SemaphoreType.DMA((2,)),
+            pltpu.SemaphoreType.DMA((3,)),
+            pltpu.SemaphoreType.DMA((3,)),
         ],
         compiler_params=pltpu.CompilerParams(
             collective_id=0, has_side_effects=True, vmem_limit_bytes=40 * 1024 * 1024
@@ -434,12 +443,11 @@
             stat_shapes,
             stat_shapes,
         ),
-        in_specs=[vmem] * 5 + [hbm],
+        in_specs=[vmem] * 6,
         out_specs=(hbm,) * 4,
         scratch_shapes=[
-            pltpu.VMEM((1, blocks), jnp.int32),
             pltpu.VMEM((blocks, entries), bf16),
-            pltpu.SemaphoreType.DMA((8,)),
+            pltpu.SemaphoreType.DMA((7,)),
         ],
         compiler_params=pltpu.CompilerParams(vmem_limit_bytes=40 * 1024 * 1024),
         cost_estimate=pl.CostEstimate(
@@ -447,14 +455,7 @@
             bytes_accessed=6 * blocks * entries + 8 * side * side,
             transcendentals=0,
         ),
-    )(
-        wide,
-        totals,
-        moment_new,
-        left_new,
-        right_new,
-        pltpu.with_memory_space_constraint(order, pltpu.HBM),
-    )
+    )(wide, totals, holds, moment_new, left_new, right_new)
     return (update, moment_new, left_new[None], right_new[None])
 
 

time: 43.3 us -> 43.1 us (level)
  no operation moved by 1% of the time
where the time goes in v5:
time: 43.1 us; the launch traced here: 43 us
  Pallas kernels  42.4 us (98%)
  between operations  0.64 us (1%)
    pallas_call x1, Pallas kernels, shards(): pl.pallas_call(functools.partial(exchange, depth, across), out_shape=(jax...  40.4 us
    pallas_call x1, Pallas kernels, shards(): pl.pallas_call(write, out_shape=(jax.ShapeDtypeStruct((blocks, entries),...  2.05 us

profile of v5, /device:TPU:1, one launch (start us, length us, event | category | flops | bytes accessed | tf_op | source)
XLA Modules:
  0.0 43.0 jit_solution(12682507369811440318)
XLA Ops:
  0.6 40.4 %shard_map.102 = (f32[2048,128]{1,0:T(8,128)S(1)}, f32[2,256]{1,0:T(2,128)S(1)}, bf16[256,256]{1,0:T(8,128)(2,1)S(1)}, f32[256,1024]{1,0:T(8,128)S(1)}, f32[512,512]{1,0:T(8,128)S(1)}, /*index=5*/f32[512,512]{1,0:T(8,128)S(1)}) custom-call(bf16[256,1024]{1,0:T(8,128)(2,1)} %grad_hbm.1, f32[256,1024]{1,0:T(8,128)} %moment_hbm.1, s32[1,256]{1,0:T(1,128)} %bitcast.11, ...), custom_call_target="tpu_custom_call" | custom-call | flops 1207959552 | bytes 4718592 | tf_op jit(solution)/shard_map/pallas_call | solution.py:375
  41.0 2.0 %shard_map.103 = (bf16[256,1024]{1,0:T(8,128)(2,1)}, f32[256,1024]{1,0:T(8,128)}, f32[512,512]{1,0:T(8,128)}, f32[512,512]{1,0:T(8,128)}) custom-call(f32[2048,128]{1,0:T(8,128)S(1)} %get-tuple-element.14.wide, f32[2,256]{1,0:T(2,128)S(1)} %get-tuple-element.15.totals, bf16[256,256]{1,0:T(8,128)(2,1)S(1)} %get-tuple-element.16.holds, ...), custom_call_target="tpu_custom_call" | custom-call | flops 134217728 | bytes 3670016 | tf_op jit(solution)/shard_map/pallas_call | solution.py:438

commit v6 on v5

--- a/solution.py
+++ b/solution.py
@@ -56,6 +56,7 @@
     via_xy,
     turned_back,
     landed_z,
+    hop,
     block,
     norms,
     norms_core,
@@ -68,6 +69,8 @@
     z_recv,
     xy_send,
     xy_recv,
+    hop_send,
+    hop_recv,
     norm_send,
     norm_recv,
 ):
@@ -146,7 +149,36 @@
         ty = lax.rem(y + j % deep, deep)
         return tx * deep + ty
 
+    hops = depth % 4 == 0
+    leg = depth // 4 + core * (depth // 2)
+
+    def send_hop(source, half):
+        pltpu.make_async_remote_copy(
+            src_ref=source.at[way, lax.rem(g + depth // 2, depth)],
+            dst_ref=hop.at[way, half],
+            send_sem=hop_send.at[way, half],
+            recv_sem=hop_recv.at[way, half],
+            device_id=(lax.rem(g + leg, depth), f),
+            device_id_type=MESH,
+        ).start()
+
+    def pass_hop(target, half):
+        if not hops:
+            return
+        wait(hop.at[way, half], hop_recv.at[way, half])
+        pltpu.make_async_remote_copy(
+            src_ref=hop.at[way, half],
+            dst_ref=target.at[way, lax.rem(g + depth - leg, depth)],
+            send_sem=z_send.at[way, half],
+            recv_sem=z_recv.at[way, half],
+            device_id=(lax.rem(g + leg, depth), f),
+            device_id_type=MESH,
+        ).start()
+
     def send_z(j, source, target, half):
+        if hops and j == depth // 2:
+            send_hop(source, half)
+            return
         to = lax.rem(g + j, depth)
         pltpu.make_async_remote_copy(
             src_ref=source.at[way, to],
@@ -188,6 +220,7 @@
         send_xy(turned_xy, via_xy, 1, 1 - core, near_first[::-1] + [0])
         for j in range(plane):
             via_z[way, g, j] = tile(g, j, core)
+        pass_hop(via_z, 0)
 
     def go_on_z():
         wait(via_xy.at[way], xy_recv.at[way, 1])
@@ -203,6 +236,7 @@
             turned_z[way, :, i] = via_z[way, i]
         send_xy(turned_z, landed_xy, 0, core, near_first[::-1])
         landed_xy[way, xy] = turned_z[way, xy]
+        pass_hop(landed_z, 1)
 
     def end(target):
         wait(landed_xy.at[way, pl.ds(0, plane - 1)], xy_recv.at[way, 0])
@@ -317,6 +351,9 @@
         wait(landed_z.at[way, pl.ds(0, depth - 1)], z_send.at[way, 1])
         wait(landed_xy.at[way, pl.ds(0, plane - 1)], xy_send.at[way, 0])
         wait(via_xy.at[way], xy_send.at[way, 1])
+        if hops:
+            for half in range(2):
+                wait(hop.at[way, half], hop_send.at[way, half])
     wait(norms_z.at[pl.ds(0, depth - 1)], norm_send.at[1])
     wait(norms_xy.at[pl.ds(0, plane - 1)], norm_send.at[2])
 
@@ -398,6 +435,7 @@
             pltpu.VMEM((2, plane, depth, *tile), bf16),
             pltpu.VMEM((2, depth, plane, *tile), bf16),
             pltpu.VMEM((2, depth, plane, *tile), bf16),
+            pltpu.VMEM((2, 2, plane, *tile), bf16),
             pltpu.VMEM((side, side), bf16),
             pltpu.VMEM((2, blocks), f32),
             pltpu.VMEM((2, blocks), f32),
@@ -406,6 +444,8 @@
             pltpu.VMEM((2, blocks), f32),
             pltpu.VMEM((plane, 2, blocks), f32),
             pltpu.SemaphoreType.DMA((7,)),
+            pltpu.SemaphoreType.DMA((2, 2)),
+            pltpu.SemaphoreType.DMA((2, 2)),
             pltpu.SemaphoreType.DMA((2, 2)),
             pltpu.SemaphoreType.DMA((2, 2)),
             pltpu.SemaphoreType.DMA((2, 2)),

time: 43.1 us -> 45.3 us (1.051)
  Pallas kernels: 42.4 us -> 44.5 us
    pallas_call x1, Pallas kernels: 40.4 us -> 42.4 us  [shards(): pl.pallas_call(functools.partial(exchange, depth, across), out_shape=(jax...]
where the time goes in v6:
time: 45.3 us; the launch traced here: 45.1 us
  Pallas kernels  44.5 us (98%)
  between operations  0.64 us (1%)
    pallas_call x1, Pallas kernels, shards(): pl.pallas_call(functools.partial(exchange, depth, across), out_shape=(jax...  42.4 us
    pallas_call x1, Pallas kernels, shards(): pl.pallas_call(write, out_shape=(jax.ShapeDtypeStruct((blocks, entries),...  2.05 us

profile of v6, /device:TPU:1, one launch (start us, length us, event | category | flops | bytes accessed | tf_op | source)
XLA Modules:
  0.0 45.1 jit_solution(7876851068265410643)
XLA Ops:
  0.6 42.4 %shard_map.102 = (f32[2048,128]{1,0:T(8,128)S(1)}, f32[2,256]{1,0:T(2,128)S(1)}, bf16[256,256]{1,0:T(8,128)(2,1)S(1)}, f32[256,1024]{1,0:T(8,128)S(1)}, f32[512,512]{1,0:T(8,128)S(1)}, /*index=5*/f32[512,512]{1,0:T(8,128)S(1)}) custom-call(bf16[256,1024]{1,0:T(8,128)(2,1)} %grad_hbm.1, f32[256,1024]{1,0:T(8,128)} %moment_hbm.1, s32[1,256]{1,0:T(1,128)} %bitcast.11, ...), custom_call_target="tpu_custom_call" | custom-call | flops 1207959552 | bytes 4718592 | tf_op jit(solution)/shard_map/pallas_call | solution.py:412
  43.0 2.0 %shard_map.103 = (bf16[256,1024]{1,0:T(8,128)(2,1)}, f32[256,1024]{1,0:T(8,128)}, f32[512,512]{1,0:T(8,128)}, f32[512,512]{1,0:T(8,128)}) custom-call(f32[2048,128]{1,0:T(8,128)S(1)} %get-tuple-element.14.wide, f32[2,256]{1,0:T(2,128)S(1)} %get-tuple-element.15.totals, bf16[256,256]{1,0:T(8,128)(2,1)S(1)} %get-tuple-element.16.holds, ...), custom_call_target="tpu_custom_call" | custom-call | flops 134217728 | bytes 3670016 | tf_op jit(solution)/shard_map/pallas_call | solution.py:478

commit v7 on v5

--- a/solution.py
+++ b/solution.py
@@ -114,8 +114,8 @@
         pl.semaphore_signal(barrier, inc=1, device_id=(g, to), device_id_type=MESH)
         return carry
 
-    lax.fori_loop(1, depth, greet_z, 0)
-    lax.fori_loop(1, fan, greet_f, 0)
+    lax.fori_loop(1, depth, greet_z, 0, unroll=True)
+    lax.fori_loop(1, fan, greet_f, 0, unroll=True)
 
     loads[0].wait()
     which = lax.broadcasted_iota(jnp.int32, (blocks, blocks), 0)
@@ -229,19 +229,24 @@
     pl.semaphore_wait(barrier, depth - 1 + fan - 1)
     begin()
 
+    def adam(first, last):
+        tall = min(blocks, 32)
+        share = jnp.zeros((1, blocks), jnp.float32)
+        for i in range(first, last, tall):
+            rows = pl.ds(i, tall)
+            gradient = grad[rows, :].astype(jnp.float32)
+            second = MOMENT_DECAY * moment[rows, :] + (1.0 - MOMENT_DECAY) * gradient * gradient
+            moment[rows, :] = second
+            direction = gradient / (jnp.sqrt(second) + ADAM_EPS)
+            squares = jnp.sum(direction * direction, axis=1, keepdims=True)
+            share = share + jnp.sum(holds[i : i + tall, :] * squares, axis=0, keepdims=True)
+        return share
+
     loads[2].wait()
-    tall = min(blocks, 32)
-    share = jnp.zeros((1, blocks), jnp.float32)
-    for i in range(0, blocks, tall):
-        rows = pl.ds(i, tall)
-        gradient = grad[rows, :].astype(jnp.float32)
-        second = MOMENT_DECAY * moment[rows, :] + (1.0 - MOMENT_DECAY) * gradient * gradient
-        moment[rows, :] = second
-        direction = gradient / (jnp.sqrt(second) + ADAM_EPS)
-        squares = jnp.sum(direction * direction, axis=1, keepdims=True)
-        share = share + jnp.sum(holds[i : i + tall, :] * squares, axis=0, keepdims=True)
-    norms[0:1, :] = share
+    split = blocks // 2 if blocks > 32 else blocks
+    norms[0:1, :] = adam(0, split)
     go_on_z()
+    norms[0:1, :] += adam(split, blocks)
     go_on_xy()
 
     end(wide)
@@ -287,13 +292,13 @@
     loads[5].wait()
     left = matmul(block[...], block[...], 1, 1)
     left_stat[...] = STAT_DECAY * left_stat[...] + (1.0 - STAT_DECAY) * left / side
+    go_on_z()
     swap.wait()
     norms_core_sum[...] = norms[...] + norms_core[...]
     lax.fori_loop(1, depth, norm_z, 0)
     loads[6].wait()
     right = matmul(block[...], block[...], 0, 0)
     right_stat[...] = STAT_DECAY * right_stat[...] + (1.0 - STAT_DECAY) * right / side
-    go_on_z()
     go_on_xy()
     wait(norms_z.at[pl.ds(0, depth - 1)], norm_recv.at[1])
     norms_z[g] = norms_core_sum[...]

time: 43.1 us -> 47.7 us (1.11)
  Pallas kernels: 42.4 us -> 47 us
    pallas_call x1, Pallas kernels: 40.4 us -> 44.9 us  [shards(): pl.pallas_call(functools.partial(exchange, depth, across), out_shape=(jax...]
where the time goes in v7:
time: 47.7 us; the launch traced here: 47.6 us
  Pallas kernels  47 us (99%)
  between operations  0.64 us (1%)
    pallas_call x1, Pallas kernels, shards(): pl.pallas_call(functools.partial(exchange, depth, across), out_shape=(jax...  44.9 us
    pallas_call x1, Pallas kernels, shards(): pl.pallas_call(write, out_shape=(jax.ShapeDtypeStruct((blocks, entries),...  2.05 us

profile of v7, /device:TPU:1, one launch (start us, length us, event | category | flops | bytes accessed | tf_op | source)
XLA Modules:
  0.0 47.6 jit_solution(17024386029633305407)
XLA Ops:
  0.6 44.9 %shard_map.102 = (f32[2048,128]{1,0:T(8,128)S(1)}, f32[2,256]{1,0:T(2,128)S(1)}, bf16[256,256]{1,0:T(8,128)(2,1)S(1)}, f32[256,1024]{1,0:T(8,128)S(1)}, f32[512,512]{1,0:T(8,128)S(1)}, /*index=5*/f32[512,512]{1,0:T(8,128)S(1)}) custom-call(bf16[256,1024]{1,0:T(8,128)(2,1)} %grad_hbm.1, f32[256,1024]{1,0:T(8,128)} %moment_hbm.1, s32[1,256]{1,0:T(1,128)} %bitcast.11, ...), custom_call_target="tpu_custom_call" | custom-call | flops 1207959552 | bytes 4718592 | tf_op jit(solution)/shard_map/pallas_call | solution.py:380
  45.5 2.0 %shard_map.103 = (bf16[256,1024]{1,0:T(8,128)(2,1)}, f32[256,1024]{1,0:T(8,128)}, f32[512,512]{1,0:T(8,128)}, f32[512,512]{1,0:T(8,128)}) custom-call(f32[2048,128]{1,0:T(8,128)S(1)} %get-tuple-element.14.wide, f32[2,256]{1,0:T(2,128)S(1)} %get-tuple-element.15.totals, bf16[256,256]{1,0:T(8,128)(2,1)S(1)} %get-tuple-element.16.holds, ...), custom_call_target="tpu_custom_call" | custom-call | flops 134217728 | bytes 3670016 | tf_op jit(solution)/shard_map/pallas_call | solution.py:443

commit v8 on v5

--- a/solution.py
+++ b/solution.py
@@ -123,99 +123,106 @@
     holds_half[...] = holds.astype(jnp.bfloat16)
     slots_half = holds.T.astype(jnp.bfloat16)
 
+    def rows_of(i, j, c):
+        return pl.ds(pl.multiple_of((i * fan + j * 2 + c) * SUBLANES, SUBLANES), SUBLANES)
+
     def tile(i, j, c):
-        first = pl.multiple_of((i * fan + j * 2 + c) * SUBLANES, SUBLANES)
-        return wide[pl.ds(first, SUBLANES), :].astype(jnp.bfloat16)
-
-    def widen(target, i, c, part):
-        part = part.astype(jnp.float32)
-        first = pl.multiple_of((i * fan + c) * SUBLANES, SUBLANES)
-        for j in range(plane):
-            target[pl.ds(first + j * 2 * SUBLANES, SUBLANES), :] = part[j]
-
-    near_first = sorted(
-        range(1, plane),
-        key=lambda j: (
-            min(j // deep, across - j // deep) + min(j % deep, deep - j % deep),
-            j,
-        ),
-    )
-
-    def place(j):
-        tx = lax.rem(x + j // deep, across)
-        ty = lax.rem(y + j % deep, deep)
-        return tx * deep + ty
-
-    def send_z(j, source, target, half):
+        return wide[rows_of(i, j, c), :].astype(jnp.bfloat16)
+
+    apart = [k for k in range(1, across, 2)] + [k for k in range(2, across, 2)] + [0]
+    part = plane // 2
+    chunks = [pl.ds(k * part, part) for k in range(2)]
+
+    def place(r, sign):
+        k = apart[r // deep]
+        return lax.rem(x + (k if sign > 0 else across - k), across) * deep + r % deep
+
+    def send_z(j, k, source, target, half):
         to = lax.rem(g + j, depth)
         pltpu.make_async_remote_copy(
-            src_ref=source.at[way, to],
-            dst_ref=target.at[way, g],
+            src_ref=source.at[way, to, chunks[k]],
+            dst_ref=target.at[way, g, chunks[k]],
             send_sem=z_send.at[way, half],
-            recv_sem=z_recv.at[way, half],
+            recv_sem=z_recv.at[way, half, k if half == 0 else 0],
             device_id=(to, f),
             device_id_type=MESH,
         ).start()
 
-    def send_xy(source, target, half, to_core, places):
-        for j in places:
-            to = place(j)
+    def send_xy(k, source, target, half, to_core, skip_self):
+        for r in range(k * part, (k + 1) * part):
+            dx = apart[r // deep]
+            turns = [j for j in (alternate(deep) + [0]) if dx or j or not skip_self]
+            if r % deep >= len(turns):
+                continue
+            to_x = lax.rem(x + dx, across)
+            to_y = lax.rem(y + turns[r % deep], deep)
+            to = to_x * deep + to_y
             pltpu.make_async_remote_copy(
-                src_ref=source.at[way, to],
-                dst_ref=target.at[way, xy],
+                src_ref=source.at[way, r // deep * deep + to_y],
+                dst_ref=target.at[way, r // deep * deep + y if half else xy],
                 send_sem=xy_send.at[way, half],
-                recv_sem=xy_recv.at[way, half],
+                recv_sem=xy_recv.at[way, half, k if half else 0],
                 device_id=(g, to * 2 + to_core),
                 device_id_type=MESH,
             ).start()
 
-    def wait(part, sem):
-        pltpu.make_async_copy(part, part, sem).wait()
+    def wait(arrived, sem):
+        pltpu.make_async_copy(arrived, arrived, sem).wait()
 
     def begin():
-        for k in alternate(depth):
-            to = lax.rem(g + k, depth)
+        for k in range(2):
+            for j in alternate(depth):
+                to = lax.rem(g + j, depth)
+                for r in range(k * part, (k + 1) * part):
+                    sent[way, to, r] = tile(to, place(r, 1), core)
+                send_z(j, k, sent, via_z, 0)
+
+            def fill(i, carry, k=k):
+                for r in range(k * part, (k + 1) * part):
+                    turned_xy[way, r, i] = tile(i, place(r, 1), 1 - core)
+                return carry
+
+            lax.fori_loop(0, depth, fill, 0)
+            send_xy(k, turned_xy, via_xy, 1, 1 - core, False)
+        for r in range(plane):
+            via_z[way, g, r] = tile(g, place(r, 1), core)
+
+    def go_on_z(k):
+        wait(via_xy.at[way, chunks[k]], xy_recv.at[way, 1, k])
+        for i in range(depth):
+            turned_back[way, i, chunks[k]] = via_xy[way, chunks[k], i]
+        for j in alternate(depth):
+            send_z(j, k, turned_back, landed_z, 1)
+
+    def go_on_xy(k):
+        wait(via_z.at[way, pl.ds(0, depth - 1), chunks[k]], z_recv.at[way, 0, k])
+        for i in range(depth):
+            turned_z[way, chunks[k], i] = via_z[way, i, chunks[k]]
+        send_xy(k, turned_z, landed_xy, 0, core, True)
+
+    def go_on():
+        for k in range(2):
+            go_on_z(k)
+            go_on_xy(k)
+        landed_z[way, g] = turned_back[way, g]
+        landed_xy[way, xy] = turned_z[way, (len(apart) - 1) * deep + y]
+
+    def end(target):
+        wait(landed_xy.at[way, pl.ds(0, plane - 1)], xy_recv.at[way, 0, 0])
+
+        def from_xy(i, carry):
+            arrived = landed_xy[way, :, i].astype(jnp.float32)
             for j in range(plane):
-                sent[way, to, j] = tile(to, j, core)
-            send_z(k, sent, via_z, 0)
-
-        def fill(i, carry):
-            for j in range(plane):
-                turned_xy[way, j, i] = tile(i, j, 1 - core)
+                target[rows_of(i, j, core), :] = arrived[j]
             return carry
 
-        lax.fori_loop(0, depth, fill, 0)
-        send_xy(turned_xy, via_xy, 1, 1 - core, near_first[::-1] + [0])
-        for j in range(plane):
-            via_z[way, g, j] = tile(g, j, core)
-
-    def go_on_z():
-        wait(via_xy.at[way], xy_recv.at[way, 1])
-        for i in range(depth):
-            turned_back[way, i] = via_xy[way, :, i]
-        for k in alternate(depth):
-            send_z(k, turned_back, landed_z, 1)
-        landed_z[way, g] = turned_back[way, g]
-
-    def go_on_xy():
-        wait(via_z.at[way, pl.ds(0, depth - 1)], z_recv.at[way, 0])
-        for i in range(depth):
-            turned_z[way, :, i] = via_z[way, i]
-        send_xy(turned_z, landed_xy, 0, core, near_first[::-1])
-        landed_xy[way, xy] = turned_z[way, xy]
-
-    def end(target):
-        wait(landed_xy.at[way, pl.ds(0, plane - 1)], xy_recv.at[way, 0])
-
-        def from_xy(i, carry):
-            widen(target, i, core, landed_xy[way, :, i])
-            return carry
-
         lax.fori_loop(0, depth, from_xy, 0)
-        wait(landed_z.at[way, pl.ds(0, depth - 1)], z_recv.at[way, 1])
+        wait(landed_z.at[way, pl.ds(0, depth - 1)], z_recv.at[way, 1, 0])
 
         def from_z(i, carry):
-            widen(target, i, 1 - core, landed_z[way, i])
+            arrived = landed_z[way, i].astype(jnp.float32)
+            for r in range(plane):
+                target[rows_of(i, place(r, -1), 1 - core), :] = arrived[r]
             return carry
 
         lax.fori_loop(0, depth, from_z, 0)
@@ -241,8 +248,7 @@
         squares = jnp.sum(direction * direction, axis=1, keepdims=True)
         share = share + jnp.sum(holds[i : i + tall, :] * squares, axis=0, keepdims=True)
     norms[0:1, :] = share
-    go_on_z()
-    go_on_xy()
+    go_on()
 
     end(wide)
     for c in range(pieces):
@@ -293,20 +299,24 @@
     loads[6].wait()
     right = matmul(block[...], block[...], 0, 0)
     right_stat[...] = STAT_DECAY * right_stat[...] + (1.0 - STAT_DECAY) * right / side
-    go_on_z()
-    go_on_xy()
+    go_on()
     wait(norms_z.at[pl.ds(0, depth - 1)], norm_recv.at[1])
     norms_z[g] = norms_core_sum[...]
     norms_z_sum[...] = jnp.sum(norms_z[...], axis=0)
-    for j in near_first:
+
+    def norm_xy(j, carry):
+        to = lax.rem(xy + j, plane)
         pltpu.make_async_remote_copy(
             src_ref=norms_z_sum,
             dst_ref=norms_xy.at[xy],
             send_sem=norm_send.at[2],
             recv_sem=norm_recv.at[2],
-            device_id=(g, place(j) * 2 + core),
+            device_id=(g, to * 2 + core),
             device_id_type=MESH,
         ).start()
+        return carry
+
+    lax.fori_loop(1, plane, norm_xy, 0)
     end(wide_back)
     wait(norms_xy.at[pl.ds(0, plane - 1)], norm_recv.at[2])
     norms_xy[xy] = norms_z_sum[...]
@@ -407,9 +417,9 @@
             pltpu.VMEM((plane, 2, blocks), f32),
             pltpu.SemaphoreType.DMA((7,)),
             pltpu.SemaphoreType.DMA((2, 2)),
+            pltpu.SemaphoreType.DMA((2, 2, 2)),
             pltpu.SemaphoreType.DMA((2, 2)),
-            pltpu.SemaphoreType.DMA((2, 2)),
-            pltpu.SemaphoreType.DMA((2, 2)),
+            pltpu.SemaphoreType.DMA((2, 2, 2)),
             pltpu.SemaphoreType.DMA((3,)),
             pltpu.SemaphoreType.DMA((3,)),
         ],

time: 43.1 us -> 42 us (0.974)
  Pallas kernels: 42.4 us -> 41.2 us
    pallas_call x1, Pallas kernels: 40.4 us -> 39.2 us  [shards(): pl.pallas_call(functools.partial(exchange, depth, across), out_shape=(jax...]
where the time goes in v8:
time: 42 us; the launch traced here: 41.9 us
  Pallas kernels  41.2 us (98%)
  between operations  0.64 us (2%)
    pallas_call x1, Pallas kernels, shards(): pl.pallas_call(functools.partial(exchange, depth, across), out_shape=(jax...  39.2 us
    pallas_call x1, Pallas kernels, shards(): pl.pallas_call(write, out_shape=(jax.ShapeDtypeStruct((blocks, entries),...  2.05 us

profile of v8, /device:TPU:1, one launch (start us, length us, event | category | flops | bytes accessed | tf_op | source)
XLA Modules:
  0.0 41.9 jit_solution(17135124951729858164)
XLA Ops:
  0.6 39.2 %shard_map.102 = (f32[2048,128]{1,0:T(8,128)S(1)}, f32[2,256]{1,0:T(2,128)S(1)}, bf16[256,256]{1,0:T(8,128)(2,1)S(1)}, f32[256,1024]{1,0:T(8,128)S(1)}, f32[512,512]{1,0:T(8,128)S(1)}, /*index=5*/f32[512,512]{1,0:T(8,128)S(1)}) custom-call(bf16[256,1024]{1,0:T(8,128)(2,1)} %grad_hbm.1, f32[256,1024]{1,0:T(8,128)} %moment_hbm.1, s32[1,256]{1,0:T(1,128)} %bitcast.11, ...), custom_call_target="tpu_custom_call" | custom-call | flops 1207959552 | bytes 4718592 | tf_op jit(solution)/shard_map/pallas_call | solution.py:385
  39.8 2.1 %shard_map.103 = (bf16[256,1024]{1,0:T(8,128)(2,1)}, f32[256,1024]{1,0:T(8,128)}, f32[512,512]{1,0:T(8,128)}, f32[512,512]{1,0:T(8,128)}) custom-call(f32[2048,128]{1,0:T(8,128)S(1)} %get-tuple-element.14.wide, f32[2,256]{1,0:T(2,128)S(1)} %get-tuple-element.15.totals, bf16[256,256]{1,0:T(8,128)(2,1)S(1)} %get-tuple-element.16.holds, ...), custom_call_target="tpu_custom_call" | custom-call | flops 134217728 | bytes 3670016 | tf_op jit(solution)/shard_map/pallas_call | solution.py:448

commit v9 on v8

--- a/solution.py
+++ b/solution.py
@@ -200,10 +200,12 @@
             turned_z[way, chunks[k], i] = via_z[way, i, chunks[k]]
         send_xy(k, turned_z, landed_xy, 0, core, True)
 
-    def go_on():
+    def go_on(between=None):
         for k in range(2):
             go_on_z(k)
             go_on_xy(k)
+            if between and k == 0:
+                between()
         landed_z[way, g] = turned_back[way, g]
         landed_xy[way, xy] = turned_z[way, (len(apart) - 1) * deep + y]
 
@@ -236,19 +238,24 @@
     pl.semaphore_wait(barrier, depth - 1 + fan - 1)
     begin()
 
+    def adam(first, last):
+        tall = min(blocks, 32)
+        share = jnp.zeros((1, blocks), jnp.float32)
+        for i in range(first, last, tall):
+            rows = pl.ds(i, tall)
+            gradient = grad[rows, :].astype(jnp.float32)
+            second = MOMENT_DECAY * moment[rows, :] + (1.0 - MOMENT_DECAY) * gradient * gradient
+            moment[rows, :] = second
+            direction = gradient / (jnp.sqrt(second) + ADAM_EPS)
+            squares = jnp.sum(direction * direction, axis=1, keepdims=True)
+            share = share + jnp.sum(holds[i : i + tall, :] * squares, axis=0, keepdims=True)
+        return share
+
     loads[2].wait()
-    tall = min(blocks, 32)
-    share = jnp.zeros((1, blocks), jnp.float32)
-    for i in range(0, blocks, tall):
-        rows = pl.ds(i, tall)
-        gradient = grad[rows, :].astype(jnp.float32)
-        second = MOMENT_DECAY * moment[rows, :] + (1.0 - MOMENT_DECAY) * gradient * gradient
-        moment[rows, :] = second
-        direction = gradient / (jnp.sqrt(second) + ADAM_EPS)
-        squares = jnp.sum(direction * direction, axis=1, keepdims=True)
-        share = share + jnp.sum(holds[i : i + tall, :] * squares, axis=0, keepdims=True)
-    norms[0:1, :] = share
+    split = blocks // 4 if blocks >= 128 else 0
+    norms[0:1, :] = adam(0, split)
     go_on()
+    norms[0:1, :] += adam(split, blocks)
 
     end(wide)
     for c in range(pieces):
@@ -290,16 +297,15 @@
         ).start()
         return carry
 
+    def sum_cores():
+        swap.wait()
+        norms_core_sum[...] = norms[...] + norms_core[...]
+        lax.fori_loop(1, depth, norm_z, 0)
+
+    go_on(sum_cores)
     loads[5].wait()
     left = matmul(block[...], block[...], 1, 1)
     left_stat[...] = STAT_DECAY * left_stat[...] + (1.0 - STAT_DECAY) * left / side
-    swap.wait()
-    norms_core_sum[...] = norms[...] + norms_core[...]
-    lax.fori_loop(1, depth, norm_z, 0)
-    loads[6].wait()
-    right = matmul(block[...], block[...], 0, 0)
-    right_stat[...] = STAT_DECAY * right_stat[...] + (1.0 - STAT_DECAY) * right / side
-    go_on()
     wait(norms_z.at[pl.ds(0, depth - 1)], norm_recv.at[1])
     norms_z[g] = norms_core_sum[...]
     norms_z_sum[...] = jnp.sum(norms_z[...], axis=0)
@@ -317,6 +323,9 @@
         return carry
 
     lax.fori_loop(1, plane, norm_xy, 0)
+    loads[6].wait()
+    right = matmul(block[...], block[...], 0, 0)
+    right_stat[...] = STAT_DECAY * right_stat[...] + (1.0 - STAT_DECAY) * right / side
     end(wide_back)
     wait(norms_xy.at[pl.ds(0, plane - 1)], norm_recv.at[2])
     norms_xy[xy] = norms_z_sum[...]

time: 42 us -> 44.8 us (1.067)
  Pallas kernels: 41.2 us -> 44.1 us
    pallas_call x1, Pallas kernels: 39.2 us -> 42 us  [shards(): pl.pallas_call(functools.partial(exchange, depth, across), out_shape=(jax...]
where the time goes in v9:
time: 44.8 us; the launch traced here: 44.7 us
  Pallas kernels  44.1 us (98%)
  between operations  0.64 us (1%)
    pallas_call x1, Pallas kernels, shards(): pl.pallas_call(functools.partial(exchange, depth, across), out_shape=(jax...  42 us
    pallas_call x1, Pallas kernels, shards(): pl.pallas_call(write, out_shape=(jax.ShapeDtypeStruct((blocks, entries),...  2.05 us

profile of v9, /device:TPU:1, one launch (start us, length us, event | category | flops | bytes accessed | tf_op | source)
XLA Modules:
  0.0 44.7 jit_solution(17601641552948151127)
XLA Ops:
  0.6 42.0 %shard_map.102 = (f32[2048,128]{1,0:T(8,128)S(1)}, f32[2,256]{1,0:T(2,128)S(1)}, bf16[256,256]{1,0:T(8,128)(2,1)S(1)}, f32[256,1024]{1,0:T(8,128)S(1)}, f32[512,512]{1,0:T(8,128)S(1)}, /*index=5*/f32[512,512]{1,0:T(8,128)S(1)}) custom-call(bf16[256,1024]{1,0:T(8,128)(2,1)} %grad_hbm.1, f32[256,1024]{1,0:T(8,128)} %moment_hbm.1, s32[1,256]{1,0:T(1,128)} %bitcast.11, ...), custom_call_target="tpu_custom_call" | custom-call | flops 1207959552 | bytes 4718592 | tf_op jit(solution)/shard_map/pallas_call | solution.py:394
  42.6 2.1 %shard_map.103 = (bf16[256,1024]{1,0:T(8,128)(2,1)}, f32[256,1024]{1,0:T(8,128)}, f32[512,512]{1,0:T(8,128)}, f32[512,512]{1,0:T(8,128)}) custom-call(f32[2048,128]{1,0:T(8,128)S(1)} %get-tuple-element.14.wide, f32[2,256]{1,0:T(2,128)S(1)} %get-tuple-element.15.totals, bf16[256,256]{1,0:T(8,128)(2,1)S(1)} %get-tuple-element.16.holds, ...), custom_call_target="tpu_custom_call" | custom-call | flops 134217728 | bytes 3670016 | tf_op jit(solution)/shard_map/pallas_call | solution.py:457

commit v10 on v8

--- a/solution.py
+++ b/solution.py
@@ -57,6 +57,7 @@
     turned_back,
     landed_z,
     block,
+    gram,
     norms,
     norms_core,
     norms_core_sum,
@@ -236,18 +237,26 @@
     pl.semaphore_wait(barrier, depth - 1 + fan - 1)
     begin()
 
+    def adam(i, share):
+        rows = pl.ds(pl.multiple_of(i * 16, 16), 16)
+        squares = jnp.zeros((16, LANES), jnp.float32)
+        for first in range(0, SUBLANES * LANES, 4 * LANES):
+            columns = pl.ds(first, 4 * LANES)
+            gradient = grad[rows, columns].astype(jnp.float32)
+            second = (
+                MOMENT_DECAY * moment[rows, columns] + (1.0 - MOMENT_DECAY) * gradient * gradient
+            )
+            moment[rows, columns] = second
+            direction = gradient / (jnp.sqrt(second) + ADAM_EPS)
+            direction = direction * direction
+            for c in range(4):
+                squares = squares + direction[:, c * LANES : (c + 1) * LANES]
+        squares = jnp.sum(squares, axis=1, keepdims=True)
+        return share + holds_half[rows, :].astype(jnp.float32) * squares
+
     loads[2].wait()
-    tall = min(blocks, 32)
-    share = jnp.zeros((1, blocks), jnp.float32)
-    for i in range(0, blocks, tall):
-        rows = pl.ds(i, tall)
-        gradient = grad[rows, :].astype(jnp.float32)
-        second = MOMENT_DECAY * moment[rows, :] + (1.0 - MOMENT_DECAY) * gradient * gradient
-        moment[rows, :] = second
-        direction = gradient / (jnp.sqrt(second) + ADAM_EPS)
-        squares = jnp.sum(direction * direction, axis=1, keepdims=True)
-        share = share + jnp.sum(holds[i : i + tall, :] * squares, axis=0, keepdims=True)
-    norms[0:1, :] = share
+    share = lax.fori_loop(0, blocks // 16, adam, jnp.zeros((16, blocks), jnp.float32))
+    norms[0:1, :] = jnp.sum(share, axis=0, keepdims=True)
     go_on()
 
     end(wide)
@@ -266,7 +275,15 @@
     begin()
 
     lane = lax.broadcasted_iota(jnp.int32, (1, blocks), 1)
-    precon_sq = jnp.sum(full * full, keepdims=True)
+
+    def add_square(i, total):
+        part = wide[pl.ds(pl.multiple_of(i * 64, 64), 64), :]
+        return total + part * part
+
+    precon_sq = lax.fori_loop(
+        0, blocks * SUBLANES // 64, add_square, jnp.zeros((64, LANES), jnp.float32)
+    )
+    precon_sq = jnp.sum(precon_sq, keepdims=True)
     norms[1:2, :] = jnp.where(lane == me, precon_sq, 0.0)
 
     swap = pltpu.make_async_remote_copy(
@@ -290,15 +307,23 @@
         ).start()
         return carry
 
+    def blend(stat):
+        def one(i, carry):
+            rows = pl.ds(pl.multiple_of(i * 16, 16), 16)
+            stat[rows, :] = STAT_DECAY * stat[rows, :] + (1.0 - STAT_DECAY) * gram[rows, :] / side
+            return carry
+
+        lax.fori_loop(0, side // 16, one, 0)
+
     loads[5].wait()
-    left = matmul(block[...], block[...], 1, 1)
-    left_stat[...] = STAT_DECAY * left_stat[...] + (1.0 - STAT_DECAY) * left / side
+    gram[...] = matmul(block[...], block[...], 1, 1)
+    blend(left_stat)
     swap.wait()
     norms_core_sum[...] = norms[...] + norms_core[...]
     lax.fori_loop(1, depth, norm_z, 0)
     loads[6].wait()
-    right = matmul(block[...], block[...], 0, 0)
-    right_stat[...] = STAT_DECAY * right_stat[...] + (1.0 - STAT_DECAY) * right / side
+    gram[...] = matmul(block[...], block[...], 0, 0)
+    blend(right_stat)
     go_on()
     wait(norms_z.at[pl.ds(0, depth - 1)], norm_recv.at[1])
     norms_z[g] = norms_core_sum[...]
@@ -409,6 +434,7 @@
             pltpu.VMEM((2, depth, plane, *tile), bf16),
             pltpu.VMEM((2, depth, plane, *tile), bf16),
             pltpu.VMEM((side, side), bf16),
+            pltpu.VMEM((side, side), f32),
             pltpu.VMEM((2, blocks), f32),
             pltpu.VMEM((2, blocks), f32),
             pltpu.VMEM((2, blocks), f32),

time: 42 us -> 42 us (level)
  no operation moved by 1% of the time
where the time goes in v10:
time: 42 us; the launch traced here: 41.9 us
  Pallas kernels  41.2 us (98%)
  between operations  0.64 us (2%)
    pallas_call x1, Pallas kernels, shards(): pl.pallas_call(functools.partial(exchange, depth, across), out_shape=(jax...  39.2 us
    pallas_call x1, Pallas kernels, shards(): pl.pallas_call(write, out_shape=(jax.ShapeDtypeStruct((blocks, entries),...  2.05 us

profile of v10, /device:TPU:1, one launch (start us, length us, event | category | flops | bytes accessed | tf_op | source)
XLA Modules:
  0.0 41.9 jit_solution(14260624118116246647)
XLA Ops:
  0.6 39.2 %shard_map.102 = (f32[2048,128]{1,0:T(8,128)S(1)}, f32[2,256]{1,0:T(2,128)S(1)}, bf16[256,256]{1,0:T(8,128)(2,1)S(1)}, f32[256,1024]{1,0:T(8,128)S(1)}, f32[512,512]{1,0:T(8,128)S(1)}, /*index=5*/f32[512,512]{1,0:T(8,128)S(1)}) custom-call(bf16[256,1024]{1,0:T(8,128)(2,1)} %grad_hbm.1, f32[256,1024]{1,0:T(8,128)} %moment_hbm.1, s32[1,256]{1,0:T(1,128)} %bitcast.11, ...), custom_call_target="tpu_custom_call" | custom-call | flops 1207959552 | bytes 4718592 | tf_op jit(solution)/shard_map/pallas_call | solution.py:410
  39.8 2.0 %shard_map.103 = (bf16[256,1024]{1,0:T(8,128)(2,1)}, f32[256,1024]{1,0:T(8,128)}, f32[512,512]{1,0:T(8,128)}, f32[512,512]{1,0:T(8,128)}) custom-call(f32[2048,128]{1,0:T(8,128)S(1)} %get-tuple-element.14.wide, f32[2,256]{1,0:T(2,128)S(1)} %get-tuple-element.15.totals, bf16[256,256]{1,0:T(8,128)(2,1)S(1)} %get-tuple-element.16.holds, ...), custom_call_target="tpu_custom_call" | custom-call | flops 134217728 | bytes 3670016 | tf_op jit(solution)/shard_map/pallas_call | solution.py:474

commit v11 on v10

--- a/solution.py
+++ b/solution.py
@@ -124,19 +124,22 @@
     holds_half[...] = holds.astype(jnp.bfloat16)
     slots_half = holds.T.astype(jnp.bfloat16)
 
-    def rows_of(i, j, c):
-        return pl.ds(pl.multiple_of((i * fan + j * 2 + c) * SUBLANES, SUBLANES), SUBLANES)
-
-    def tile(i, j, c):
-        return wide[rows_of(i, j, c), :].astype(jnp.bfloat16)
+    def first_of(i, tx, c):
+        return pl.multiple_of((i * fan + tx * (deep * 2) + c) * SUBLANES, SUBLANES)
+
+    def rows_of(first, j):
+        return pl.ds(first + j * (2 * SUBLANES), SUBLANES)
+
+    def tile(first, j):
+        return wide[rows_of(first, j), :].astype(jnp.bfloat16)
 
     apart = [k for k in range(1, across, 2)] + [k for k in range(2, across, 2)] + [0]
     part = plane // 2
     chunks = [pl.ds(k * part, part) for k in range(2)]
 
-    def place(r, sign):
+    def across_by(r, sign):
         k = apart[r // deep]
-        return lax.rem(x + (k if sign > 0 else across - k), across) * deep + r % deep
+        return lax.rem(x + (k if sign > 0 else across - k), across)
 
     def send_z(j, k, source, target, half):
         to = lax.rem(g + j, depth)
@@ -174,19 +177,25 @@
         for k in range(2):
             for j in alternate(depth):
                 to = lax.rem(g + j, depth)
-                for r in range(k * part, (k + 1) * part):
-                    sent[way, to, r] = tile(to, place(r, 1), core)
+                for r in range(k * part, (k + 1) * part, deep):
+                    first = first_of(to, across_by(r, 1), core)
+                    for i in range(deep):
+                        sent[way, to, r + i] = tile(first, i)
                 send_z(j, k, sent, via_z, 0)
 
             def fill(i, carry, k=k):
-                for r in range(k * part, (k + 1) * part):
-                    turned_xy[way, r, i] = tile(i, place(r, 1), 1 - core)
+                for r in range(k * part, (k + 1) * part, deep):
+                    first = first_of(i, across_by(r, 1), 1 - core)
+                    for j in range(deep):
+                        turned_xy[way, r + j, i] = tile(first, j)
                 return carry
 
             lax.fori_loop(0, depth, fill, 0)
             send_xy(k, turned_xy, via_xy, 1, 1 - core, False)
-        for r in range(plane):
-            via_z[way, g, r] = tile(g, place(r, 1), core)
+        for r in range(0, plane, deep):
+            first = first_of(g, across_by(r, 1), core)
+            for i in range(deep):
+                via_z[way, g, r + i] = tile(first, i)
 
     def go_on_z(k):
         wait(via_xy.at[way, chunks[k]], xy_recv.at[way, 1, k])
@@ -213,8 +222,9 @@
 
         def from_xy(i, carry):
             arrived = landed_xy[way, :, i].astype(jnp.float32)
+            first = first_of(i, 0, core)
             for j in range(plane):
-                target[rows_of(i, j, core), :] = arrived[j]
+                target[rows_of(first, j), :] = arrived[j]
             return carry
 
         lax.fori_loop(0, depth, from_xy, 0)
@@ -222,8 +232,10 @@
 
         def from_z(i, carry):
             arrived = landed_z[way, i].astype(jnp.float32)
-            for r in range(plane):
-                target[rows_of(i, place(r, -1), 1 - core), :] = arrived[r]
+            for r in range(0, plane, deep):
+                first = first_of(i, across_by(r, -1), 1 - core)
+                for j in range(deep):
+                    target[rows_of(first, j), :] = arrived[r + j]
             return carry
 
         lax.fori_loop(0, depth, from_z, 0)
@@ -370,11 +382,16 @@
     update,
     sems,
 ):
-    stores = [
-        pltpu.make_async_copy(moment, moment_hbm, sems.at[0]),
-        pltpu.make_async_copy(left_stat, left_hbm, sems.at[1]),
-        pltpu.make_async_copy(right_stat, right_hbm, sems.at[2]),
-    ]
+    stores = []
+    for i, (source, target) in enumerate(
+        ((moment, moment_hbm), (left_stat, left_hbm), (right_stat, right_hbm))
+    ):
+        quarter = source.shape[0] // 4
+        for j in range(4):
+            rows = pl.ds(j * quarter, quarter)
+            stores.append(
+                pltpu.make_async_copy(source.at[rows], target.at[rows], sems.at[i * 4 + j])
+            )
     for store in stores:
         store.start()
     blocks = update.shape[0]
@@ -387,7 +404,7 @@
         columns = pl.ds(c * LANES, 2 * LANES)
         update[:, columns] = (matmul(holds[...], pair) * scale).astype(jnp.bfloat16)
         stores.append(
-            pltpu.make_async_copy(update.at[:, columns], update_hbm.at[:, columns], sems.at[3 + c // 2])
+            pltpu.make_async_copy(update.at[:, columns], update_hbm.at[:, columns], sems.at[12 + c // 2])
         )
         stores[-1].start()
     for store in stores:
@@ -483,7 +500,7 @@
         out_specs=(hbm,) * 4,
         scratch_shapes=[
             pltpu.VMEM((blocks, entries), bf16),
-            pltpu.SemaphoreType.DMA((7,)),
+            pltpu.SemaphoreType.DMA((16,)),
         ],
         compiler_params=pltpu.CompilerParams(vmem_limit_bytes=40 * 1024 * 1024),
         cost_estimate=pl.CostEstimate(

time: 42 us -> 42 us (level)
  no operation moved by 1% of the time
where the time goes in v11:
time: 42 us; the launch traced here: 41.9 us
  Pallas kernels  41.3 us (98%)
  between operations  0.64 us (2%)
    pallas_call x1, Pallas kernels, shards(): pl.pallas_call(functools.partial(exchange, depth, across), out_shape=(jax...  39.2 us
    pallas_call x1, Pallas kernels, shards(): pl.pallas_call(write, out_shape=(jax.ShapeDtypeStruct((blocks, entries),...  2.09 us

profile of v11, /device:TPU:1, one launch (start us, length us, event | category | flops | bytes accessed | tf_op | source)
XLA Modules:
  0.0 41.9 jit_solution(18202983266824956852)
XLA Ops:
  0.6 39.2 %shard_map.102 = (f32[2048,128]{1,0:T(8,128)S(1)}, f32[2,256]{1,0:T(2,128)S(1)}, bf16[256,256]{1,0:T(8,128)(2,1)S(1)}, f32[256,1024]{1,0:T(8,128)S(1)}, f32[512,512]{1,0:T(8,128)S(1)}, /*index=5*/f32[512,512]{1,0:T(8,128)S(1)}) custom-call(bf16[256,1024]{1,0:T(8,128)(2,1)} %grad_hbm.1, f32[256,1024]{1,0:T(8,128)} %moment_hbm.1, s32[1,256]{1,0:T(1,128)} %bitcast.11, ...), custom_call_target="tpu_custom_call" | custom-call | flops 1207959552 | bytes 4718592 | tf_op jit(solution)/shard_map/pallas_call | solution.py:427
  39.8 2.1 %shard_map.103 = (bf16[256,1024]{1,0:T(8,128)(2,1)}, f32[256,1024]{1,0:T(8,128)}, f32[512,512]{1,0:T(8,128)}, f32[512,512]{1,0:T(8,128)}) custom-call(f32[2048,128]{1,0:T(8,128)S(1)} %get-tuple-element.14.wide, f32[2,256]{1,0:T(2,128)S(1)} %get-tuple-element.15.totals, bf16[256,256]{1,0:T(8,128)(2,1)S(1)} %get-tuple-element.16.holds, ...), custom_call_target="tpu_custom_call" | custom-call | flops 134217728 | bytes 3670016 | tf_op jit(solution)/shard_map/pallas_call | solution.py:491

commit v12 on v10

--- a/solution.py
+++ b/solution.py
@@ -172,19 +172,19 @@
 
     def begin():
         for k in range(2):
+            def fill(i, carry, k=k):
+                for r in range(k * part, (k + 1) * part):
+                    turned_xy[way, r, i] = tile(i, place(r, 1), 1 - core)
+                return carry
+
+            lax.fori_loop(0, depth, fill, 0)
+            send_xy(k, turned_xy, via_xy, 1, 1 - core, False)
+
             for j in alternate(depth):
                 to = lax.rem(g + j, depth)
                 for r in range(k * part, (k + 1) * part):
                     sent[way, to, r] = tile(to, place(r, 1), core)
                 send_z(j, k, sent, via_z, 0)
-
-            def fill(i, carry, k=k):
-                for r in range(k * part, (k + 1) * part):
-                    turned_xy[way, r, i] = tile(i, place(r, 1), 1 - core)
-                return carry
-
-            lax.fori_loop(0, depth, fill, 0)
-            send_xy(k, turned_xy, via_xy, 1, 1 - core, False)
         for r in range(plane):
             via_z[way, g, r] = tile(g, place(r, 1), core)
 

time: 42 us -> 42.2 us (level)
  no operation moved by 1% of the time
where the time goes in v12:
time: 42.2 us; the launch traced here: 42.1 us
  Pallas kernels  41.5 us (98%)
  between operations  0.64 us (2%)
    pallas_call x1, Pallas kernels, shards(): pl.pallas_call(functools.partial(exchange, depth, across), out_shape=(jax...  39.4 us
    pallas_call x1, Pallas kernels, shards(): pl.pallas_call(write, out_shape=(jax.ShapeDtypeStruct((blocks, entries),...  2.05 us

profile of v12, /device:TPU:1, one launch (start us, length us, event | category | flops | bytes accessed | tf_op | source)
XLA Modules:
  0.0 42.1 jit_solution(15862917955253360817)
XLA Ops:
  0.6 39.4 %shard_map.102 = (f32[2048,128]{1,0:T(8,128)S(1)}, f32[2,256]{1,0:T(2,128)S(1)}, bf16[256,256]{1,0:T(8,128)(2,1)S(1)}, f32[256,1024]{1,0:T(8,128)S(1)}, f32[512,512]{1,0:T(8,128)S(1)}, /*index=5*/f32[512,512]{1,0:T(8,128)S(1)}) custom-call(bf16[256,1024]{1,0:T(8,128)(2,1)} %grad_hbm.1, f32[256,1024]{1,0:T(8,128)} %moment_hbm.1, s32[1,256]{1,0:T(1,128)} %bitcast.11, ...), custom_call_target="tpu_custom_call" | custom-call | flops 1207959552 | bytes 4718592 | tf_op jit(solution)/shard_map/pallas_call | solution.py:410
  40.1 2.0 %shard_map.103 = (bf16[256,1024]{1,0:T(8,128)(2,1)}, f32[256,1024]{1,0:T(8,128)}, f32[512,512]{1,0:T(8,128)}, f32[512,512]{1,0:T(8,128)}) custom-call(f32[2048,128]{1,0:T(8,128)S(1)} %get-tuple-element.14.wide, f32[2,256]{1,0:T(2,128)S(1)} %get-tuple-element.15.totals, bf16[256,256]{1,0:T(8,128)(2,1)S(1)} %get-tuple-element.16.holds, ...), custom_call_target="tpu_custom_call" | custom-call | flops 134217728 | bytes 3670016 | tf_op jit(solution)/shard_map/pallas_call | solution.py:474

commit v13 on v10

--- a/solution.py
+++ b/solution.py
@@ -120,9 +120,9 @@
 
     loads[0].wait()
     which = lax.broadcasted_iota(jnp.int32, (blocks, blocks), 0)
-    holds = jnp.where(which == order[...], 1.0, 0.0)
-    holds_half[...] = holds.astype(jnp.bfloat16)
-    slots_half = holds.T.astype(jnp.bfloat16)
+    holds = jnp.where(which == order[...], 1.0, 0.0).astype(jnp.bfloat16)
+    holds_half[...] = holds
+    slots_half = holds.T
 
     def rows_of(i, j, c):
         return pl.ds(pl.multiple_of((i * fan + j * 2 + c) * SUBLANES, SUBLANES), SUBLANES)

time: 42 us -> 42 us (level)
  no operation moved by 1% of the time
where the time goes in v13:
time: 42 us; the launch traced here: 41.9 us
  Pallas kernels  41.2 us (98%)
  between operations  0.64 us (2%)
    pallas_call x1, Pallas kernels, shards(): pl.pallas_call(functools.partial(exchange, depth, across), out_shape=(jax...  39.2 us
    pallas_call x1, Pallas kernels, shards(): pl.pallas_call(write, out_shape=(jax.ShapeDtypeStruct((blocks, entries),...  2.05 us

profile of v13, /device:TPU:1, one launch (start us, length us, event | category | flops | bytes accessed | tf_op | source)
XLA Modules:
  0.0 41.9 jit_solution(12381900966647282628)
XLA Ops:
  0.6 39.2 %shard_map.102 = (f32[2048,128]{1,0:T(8,128)S(1)}, f32[2,256]{1,0:T(2,128)S(1)}, bf16[256,256]{1,0:T(8,128)(2,1)S(1)}, f32[256,1024]{1,0:T(8,128)S(1)}, f32[512,512]{1,0:T(8,128)S(1)}, /*index=5*/f32[512,512]{1,0:T(8,128)S(1)}) custom-call(bf16[256,1024]{1,0:T(8,128)(2,1)} %grad_hbm.1, f32[256,1024]{1,0:T(8,128)} %moment_hbm.1, s32[1,256]{1,0:T(1,128)} %bitcast.11, ...), custom_call_target="tpu_custom_call" | custom-call | flops 1207959552 | bytes 4718592 | tf_op jit(solution)/shard_map/pallas_call | solution.py:410
  39.8 2.0 %shard_map.103 = (bf16[256,1024]{1,0:T(8,128)(2,1)}, f32[256,1024]{1,0:T(8,128)}, f32[512,512]{1,0:T(8,128)}, f32[512,512]{1,0:T(8,128)}) custom-call(f32[2048,128]{1,0:T(8,128)S(1)} %get-tuple-element.14.wide, f32[2,256]{1,0:T(2,128)S(1)} %get-tuple-element.15.totals, bf16[256,256]{1,0:T(8,128)(2,1)S(1)} %get-tuple-element.16.holds, ...), custom_call_target="tpu_custom_call" | custom-call | flops 134217728 | bytes 3670016 | tf_op jit(solution)/shard_map/pallas_call | solution.py:474
